TPU v7x, 32 devices: a whole 2x2x4 slice. The times are simulated.
32 devices in a mesh: row: 8 (over z, core), col: 4 (over y, x).
Axes of the slice: x: 2, y: 2, z: 4, core: 2. Of those that a mesh axis runs over, the one named last changes fastest.
Arguments:
- covariance: float32 [8192, 8192], P('row', 'col')
- lon_speed: float32 [8192], replicated, may hold values from 0.05 to 0.45
- lat_speed: float32 [8192], replicated, may hold values from 0.05 to 0.45
- lon_sign: int32 [8192], replicated, may hold values from 0 to 1
- lat_sign: int32 [8192], replicated, may hold values from 0 to 1
- measurement_site_position: int32 [256], replicated, may hold values from 0 to 8191, as said below
- obs_var: float32 [256], replicated, may hold values from 0.5 to 2
Outputs:
- analysis: float32 [8192, 8192], P('row', 'col')
Inputs may be any that keep to these rules, and one draw needn't show every extreme that they name: `measurement_site_position`: distinct cells.
All inputs are finite; a program needn't handle non-finite values.
Results may differ from a plain program's by a relative error of at most 0.00012.
Values sent between devices are 32-bit elements; how exact they have to be, the bound alone decides.
A program may use at most 128 MiB of HBM per device.

v0:
```python
import jax
import jax.numpy as jnp
from jax import lax
from jax.sharding import PartitionSpec as P

PARALLEL_STRIPS = 64
MERIDIAN_TOTAL = 128
STEPS = 3


def padded_2(cells, sides, width):
    for axis, dim in sides:
        count = lax.axis_size(axis)
        ends = count - 1
        head = lax.slice_in_dim(cells, 0, width, axis=dim)
        tail = lax.slice_in_dim(cells, cells.shape[dim] - width, cells.shape[dim], axis=dim)
        cells = jnp.concatenate(
            [
                lax.ppermute(tail, axis, [(i, (i + 1) % count) for i in range(ends)]),
                cells,
                lax.ppermute(head, axis, [((i + 1) % count, i) for i in range(ends)]),
            ],
            axis=dim,
        )
    return cells


def advect(q, minus, plus, cu, cv, su, sv, lat_axis):
    lon_up = jnp.where(su > 0, jnp.roll(q, 1, lat_axis + 1), jnp.roll(q, -1, lat_axis + 1))
    lat_up = jnp.where(sv > 0, minus, plus)
    return q - cu * (q - lon_up) - cv * (q - lat_up)


def shards(
    covariance, lon_speed, lat_speed, lon_sign, lat_sign, measurement_site_position, obs_var
):
    rows_dev, cols_dev = covariance.shape
    row_bands = rows_dev // MERIDIAN_TOTAL
    col_bands = cols_dev // MERIDIAN_TOTAL
    row_start = lax.axis_index("row") * rows_dev
    col_start = lax.axis_index("col") * cols_dev

    def row_coeff(field):
        return lax.dynamic_slice_in_dim(field, row_start, rows_dev).reshape(
            row_bands, MERIDIAN_TOTAL, 1
        )

    row_cu, row_cv = (row_coeff(lon_speed), row_coeff(lat_speed))
    row_su, row_sv = (row_coeff(lon_sign), row_coeff(lat_sign))
    segment_patch = covariance
    for step in range(STEPS):
        padded = padded_2(segment_patch, (("row", 0),), MERIDIAN_TOTAL)
        shaped = padded.reshape(row_bands + 2, MERIDIAN_TOTAL, cols_dev)
        segment_patch = advect(
            shaped[1:-1], shaped[:-2], shaped[2:], row_cu, row_cv, row_su, row_sv, 0
        )
        segment_patch = segment_patch.reshape(rows_dev, cols_dev)
    margin = STEPS * MERIDIAN_TOTAL
    total_bands = col_bands + 2 * STEPS

    def wide_coeff(field):
        extended = jnp.pad(field, (margin, margin))
        return lax.dynamic_slice_in_dim(extended, col_start, cols_dev + 2 * margin).reshape(
            1, total_bands, MERIDIAN_TOTAL
        )

    col_cu, col_cv = (wide_coeff(lon_speed), wide_coeff(lat_speed))
    col_su, col_sv = (wide_coeff(lon_sign), wide_coeff(lat_sign))
    band_ids = col_start // MERIDIAN_TOTAL - STEPS + jnp.arange(total_bands, dtype=jnp.int32)
    inside = (
        ((band_ids >= 0) & (band_ids < PARALLEL_STRIPS))
        .astype(jnp.float32)
        .reshape(1, total_bands, 1)
    )
    padded = padded_2(segment_patch, (("col", 1),), margin)
    current = padded.reshape(rows_dev, total_bands, MERIDIAN_TOTAL)
    offset = 0
    for step in range(STEPS):
        count = current.shape[1]
        low, high = (offset + 1, offset + count - 1)
        current = (
            advect(
                current[:, 1:-1],
                current[:, :-2],
                current[:, 2:],
                col_cu[:, low:high],
                col_cv[:, low:high],
                col_su[:, low:high],
                col_sv[:, low:high],
                1,
            )
            * inside[:, low:high]
        )
        offset = offset + 1
    segment_patch = current.reshape(rows_dev, cols_dev)
    col_local = measurement_site_position - col_start
    row_local = measurement_site_position - row_start
    col_valid = (col_local >= 0) & (col_local < cols_dev)
    row_valid = (row_local >= 0) & (row_local < rows_dev)
    col_clip = jnp.clip(col_local, 0, cols_dev - 1)
    row_clip = jnp.clip(row_local, 0, rows_dev - 1)
    highest = lax.Precision.HIGHEST
    pht_local = jnp.where(col_valid[None, :], jnp.take(segment_patch, col_clip, axis=1), 0.0)
    hp_local = jnp.where(row_valid[:, None], jnp.take(segment_patch, row_clip, axis=0), 0.0)
    background_product_gain = lax.psum(pht_local, "col")
    inner_local = jnp.where(
        row_valid[:, None], jnp.take(background_product_gain, row_clip, axis=0), 0.0
    )
    measured_background_lines, hpht = lax.psum((hp_local, inner_local), "row")
    innovation = hpht + jnp.diag(obs_var)
    factor = jnp.linalg.cholesky(innovation)
    weights = jax.scipy.linalg.cho_solve((factor, True), measured_background_lines)
    measurement_correction = jnp.dot(
        background_product_gain, weights, precision=highest, preferred_element_type=jnp.float32
    )
    return segment_patch - measurement_correction


def solution(mesh):
    return jax.shard_map(
        shards,
        mesh=mesh,
        in_specs=(P("row", "col"), P(), P(), P(), P(), P(), P()),
        out_specs=P("row", "col"),
        check_vma=False,
    )
```

profile of v0, /device:TPU:0, one launch (start us, length us, event | category | flops | bytes accessed | tf_op | source)
XLA Modules:
  0.0 571.9 jit_solution(9145035044836264625)
XLA Ops:
  24.2 13.3 %fusion.73 = (f32[8,127,2048]{2,1,0:T(8,128)}, f32[8,127,2048]{2,1,0:T(8,128)}) fusion(f32[8,128,2048]{2,1,0:T(8,128)} %bitcast.136), kind=kLoop, calls=%fused_computation.160 | loop fusion | bytes 33292288 | tf_op jit(solution)/shard_map/jit(_roll_static)/slice | solution.py:29
  37.5 11.0 %pad_maximum_fusion.5 = (f32[1024,2048]{1,0:T(8,128)}, f32[1024,2048]{1,0:T(8,128)}) fusion(f32[128,2048]{1,0:T(8,128)S(1)} %collective-permute-done.1, f32[1024,2048]{1,0:T(8,128)} %param.7, f32[128,2048]{1,0:T(8,128)S(1)} %collective-permute-done), kind=kLoop, calls=%fused_computation.37 | loop fusion | flops 4194304 | bytes 27262976 | tf_op jit(solution)/shard_map/concatenate | solution.py:17
  48.6 19.6 %multiply_subtract_fusion.1 = (f32[8,128,2048]{2,1,0:T(8,128)}, f32[8,128,2048]{2,1,0:T(8,128)}, f32[8,128,2048]{2,1,0:T(8,128)}) fusion(f32[8,128,2048]{2,1,0:T(8,128)S(1)} %bitcast.139, f32[8,128,2048]{2,1,0:T(8,128)} %bitcast.149, f32[8,128,2048]{2,1,0:T(8,128)} %bitcast.148, f32[8,128]{1,0:T(8,128)S(1)} %dynamic-slice_bitcast_fusion.1, ...), kind=kLoop, calls=%fused_computation.64 | loop fusion | flops 20971520 | bytes 67119104 | tf_op jit(solution)/shard_map/sub | solution.py:31
  80.0 12.7 %fusion.35 = f32[1024,2048]{1,0:T(8,128)} fusion(f32[1024,2048]{1,0:T(8,128)S(1)} %bitcast.138, f32[8,128,2048]{2,1,0:T(8,128)} %get-tuple-element.44, f32[8,128,2048]{2,1,0:T(8,128)} %get-tuple-element.43, f32[1024]{0:T(1024)S(1)} %dynamic_slice.26, f32[1024]{0:T(1024)S(1)} %dynamic_slice.24, pred[1024]{0:T(1024)(128)(4,1)S(1)} %get-tuple-element.91, ...), kind=kLoop, calls=%fused_computation.62 | loop fusion | flops 20971520 | bytes 35661824 | tf_op jit(solution)/shard_map/sub | solution.py:31
  92.7 13.1 %fusion.71 = (f32[8,127,2048]{2,1,0:T(8,128)}, f32[8,127,2048]{2,1,0:T(8,128)}) fusion(f32[8,128,2048]{2,1,0:T(8,128)} %get-tuple-element.42), kind=kLoop, calls=%fused_computation.158 | loop fusion | bytes 33292288 | tf_op jit(solution)/shard_map/jit(_roll_static)/slice | solution.py:29
  105.8 10.8 %pad_maximum_fusion.3 = (f32[1024,2048]{1,0:T(8,128)}, f32[1024,2048]{1,0:T(8,128)}) fusion(f32[128,2048]{1,0:T(8,128)} %collective-permute-done.3, f32[1024,2048]{1,0:T(8,128)} %fusion.35, f32[128,2048]{1,0:T(8,128)} %collective-permute-done.2), kind=kLoop, calls=%fused_computation.35 | loop fusion | flops 4194304 | bytes 27262976 | tf_op jit(solution)/shard_map/concatenate | solution.py:17
  116.6 17.5 %multiply_subtract_fusion = (f32[8,128,2048]{2,1,0:T(8,128)S(1)}, f32[8,128,2048]{2,1,0:T(8,128)}, f32[8,128,2048]{2,1,0:T(8,128)}) fusion(f32[8,128,2048]{2,1,0:T(8,128)S(1)} %bitcast.141, f32[8,128,2048]{2,1,0:T(8,128)} %bitcast.147, f32[8,128,2048]{2,1,0:T(8,128)} %bitcast.146, f32[8,128]{1,0:T(8,128)S(1)} %dynamic-slice_bitcast_fusion.1, ...), kind=kLoop, calls=%fused_computation.63 | loop fusion | flops 20971520 | bytes 67119104 | tf_op jit(solution)/shard_map/sub | solution.py:31
  157.3 12.7 %fusion.31 = f32[1024,2048]{1,0:T(8,128)} fusion(f32[1024,2048]{1,0:T(8,128)S(1)} %bitcast.143, f32[8,128,2048]{2,1,0:T(8,128)} %get-tuple-element.41, f32[8,128,2048]{2,1,0:T(8,128)} %get-tuple-element.40, f32[1024]{0:T(1024)S(1)} %dynamic_slice.26, f32[1024]{0:T(1024)S(1)} %dynamic_slice.24, pred[1024]{0:T(1024)(128)(4,1)S(1)} %get-tuple-element.91, ...), kind=kLoop, calls=%fused_computation.57 | loop fusion | flops 20971520 | bytes 35661824 | tf_op jit(solution)/shard_map/sub | solution.py:31
  170.0 14.7 %fusion.21 = f32[1024,2048]{1,0:T(8,128)S(1)} fusion(f32[1024,2048]{1,0:T(8,128)} %fusion.31, f32[128,2048]{1,0:T(8,128)} %collective-permute-done.5, f32[128,2048]{1,0:T(8,128)S(1)} %collective-permute-done.4, f32[8,128,2048]{2,1,0:T(8,128)} %pad_maximum_fusion.12, f32[8,128,2048]{2,1,0:T(8,128)} %pad_maximum_fusion.11, f32[1024]{0:T(1024)S(1)} %dynamic_slice.26, ...), kind=kLoop, calls=%fused_computation.33 | loop fusion | flops 20971520 | bytes 35661824 | tf_op jit(solution)/shard_map/sub | solution.py:31
  190.3 31.5 %collective-permute-done.6 = f32[1024,384]{1,0:T(8,128)S(1)} collective-permute-done((f32[1024,384]{1,0:T(8,128)S(1)}, f32[1024,384]{1,0:T(8,128)S(1)}, u32[]{:S(2)}, u32[]{:S(2)}) %collective-permute-start.6) | collective-permute-done | bytes 1572896 | tf_op jit(solution)/shard_map/ppermute | solution.py:19
  221.8 35.7 %collective-permute-done.7 = f32[1024,384]{1,0:T(8,128)S(1)} collective-permute-done((f32[1024,384]{1,0:T(8,128)S(1)}, f32[1024,384]{1,0:T(8,128)S(1)}, u32[]{:S(2)}, u32[]{:S(2)}) %collective-permute-start.7) | collective-permute-done | bytes 1572896 | tf_op jit(solution)/shard_map/ppermute | solution.py:21
  262.0 12.0 %copy.32 = f32[1024,2816]{0,1:T(8,128)} copy(f32[1024,2816]{1,0:T(8,128)} %pad_maximum_fusion) | data formatting | bytes 23068672 | tf_op jit(solution)/shard_map/concatenate | solution.py:17
  274.0 20.1 %fusion.62 = (f32[1024,20,127]{0,2,1:T(8,128)}, f32[1024,20,127]{0,2,1:T(8,128)}) fusion(f32[1024,22,128]{0,2,1:T(8,128)} %bitcast.132), kind=kLoop, calls=%fused_computation.149 | loop fusion | bytes 41615360 | tf_op jit(solution)/shard_map/jit(_roll_static)/slice | solution.py:29
  294.2 13.4 %fusion.3 = f32[1024,20,128]{0,2,1:T(8,128)S(1)} fusion(f32[1024,22,128]{0,2,1:T(8,128)S(1)} %bitcast.134, f32[1024,20,127]{0,2,1:T(8,128)} %get-tuple-element.48, f32[1024,20,1]{0,2,1:T(1,128)S(1)} %get-tuple-element.50, f32[1024,20,1]{0,2,1:T(1,128)S(1)} %get-tuple-element.49, f32[1024,20,127]{0,2,1:T(8,128)} %get-tuple-element.47, ...), kind=kLoop, calls=%fused_computation.10 | loop fusion | flops 28835840 | bytes 62940240 | tf_op jit(solution)/shard_map/mul | solution.py:82
  315.4 13.0 %fusion.10 = f32[1024,18,128]{0,2,1:T(8,128)} fusion(f32[1024,20,128]{0,2,1:T(8,128)S(1)} %fusion.3, f32[1024,18,127]{0,2,1:T(8,128)} %get-tuple-element.52, f32[1024,18,1]{0,2,1:T(1,128)S(1)} %get-tuple-element.54, f32[1024,18,1]{0,2,1:T(1,128)S(1)} %get-tuple-element.53, f32[1024,18,127]{0,2,1:T(8,128)} %get-tuple-element.51, f32[18]{0:T(128)S(1)} %copy-done.15, ...), kind=kLoop, calls=%fused_computation.19 | loop fusion | flops 25952256 | bytes 56646216 | tf_op jit(solution)/shard_map/mul | solution.py:82
  328.3 10.8 %fusion.66 = (f32[1024,16,127]{0,2,1:T(8,128)S(1)}, f32[1024,16,127]{0,2,1:T(8,128)}) fusion(f32[1024,18,128]{0,2,1:T(8,128)} %fusion.10), kind=kLoop, calls=%fused_computation.153 | loop fusion | bytes 33292288 | tf_op jit(solution)/shard_map/jit(_roll_static)/slice | solution.py:29
  339.3 9.4 %fusion.17 = f32[1024,16,128]{0,2,1:T(8,128)} fusion(f32[1024,18,128]{0,2,1:T(8,128)S(1)} %copy-done.1, f32[1024,16,127]{0,2,1:T(8,128)} %get-tuple-element.56, f32[1024,16,1]{0,2,1:T(1,128)S(1)} %get-tuple-element.58, f32[1024,16,1]{0,2,1:T(1,128)S(1)} %get-tuple-element.57, f32[1024,16,127]{0,2,1:T(8,128)S(1)} %get-tuple-element.55, f32[16]{0:T(128)S(1)} %copy-done.14, ...), kind=kLoop, calls=%fused_computation.28 | loop fusion | flops 23068672 | bytes 50352192 | tf_op jit(solution)/shard_map/mul | solution.py:82
  371.7 38.6 %all-reduce.9.cloned.1.call-done = f32[1024,256]{0,1:T(8,128)} async-done(((f32[1024,256]{0,1:T(8,128)}), f32[1024,256]{0,1:T(8,128)}) %all-reduce.9.cloned.1.call-update) | async-done | bytes 1048592 | tf_op jit(solution)/shard_map/psum | solution.py:105
  413.7 67.1 %all-reduce.11.cloned.1.call-done = (f32[256,2048]{1,0:T(8,128)}, f32[256,256]{0,1:T(8,128)}) async-done(((f32[256,2048]{1,0:T(8,128)}, f32[256,256]{0,1:T(8,128)}), (f32[256,2048]{1,0:T(8,128)}, f32[256,256]{0,1:T(8,128)})) %all-reduce.11.cloned.1.call-update) | async-done | bytes 2359312 | tf_op jit(solution)/shard_map/psum | solution.py:109
  483.1 11.7 %cholesky.48 = f32[128,128]{1,0:T(8,128)S(1)} custom-call(f32[128,128]{1,0:T(8,128)S(1)} %cholesky.112), custom_call_target="Cholesky" | custom-call | tf_op jit(solution)/shard_map/jit(cholesky)/cholesky | solution.py:111
  494.9 9.8 %custom-call.18 = f32[1,128,128]{1,2,0:T(8,128)S(1)} custom-call(f32[1,128,128]{2,1,0:T(8,128)S(1)} %get-tuple-element.84), custom_call_target="InvertDiagBlocksLowerTriangular" | custom-call | tf_op jit(solution)/shard_map/jit(cholesky)/cholesky | solution.py:111
  505.2 11.9 %cholesky.101 = f32[128,128]{1,0:T(8,128)S(1)} custom-call(f32[128,128]{1,0:T(8,128)S(1)} %convolution_subtract_fusion.3), custom_call_target="Cholesky" | custom-call | tf_op jit(solution)/shard_map/jit(cholesky)/cholesky | solution.py:111
  525.1 20.5 %custom-call.19 = f32[2,128,128]{1,2,0:T(8,128)S(1)} custom-call(f32[2,128,128]{2,1,0:T(8,128)} %get-tuple-element.12), custom_call_target="InvertDiagBlocksLowerTriangular" | custom-call | tf_op jit(solution)/shard_map/jit(_cho_solve)/triangular_solve | solution.py:112
  553.1 11.5 %convolution_subtract_fusion = f32[1024,2048]{1,0:T(8,128)} fusion(f32[1024,2048]{1,0:T(8,128)} %copy.42, f32[1024,256]{0,1:T(8,128)S(1)} %copy-done.2, f32[128,2048]{1,0:T(8,128)S(1)} %fusion.46, f32[128,2048]{1,0:T(8,128)S(1)} %fusion.45), kind=kOutput, calls=%fused_computation.65 | convolution fusion | flops 6445072384 | bytes 19922944 | tf_op jit(solution)/shard_map/dot_general | solution.py:113
  (152 shorter events, 119.0 us)
Async XLA Ops:
  6.5 403.8 %all-reduce.9.cloned.1.call-start = ((), (), s32[]{:S(2)}) async-start(), calls=%async_computation | async-start | bytes 2097152 | tf_op jit(solution)/shard_map/psum | solution.py:105
  9.6 27.9 %collective-permute-start = (f32[128,2048]{1,0:T(8,128)}, f32[128,2048]{1,0:T(8,128)S(1)}, u32[]{:S(2)}, u32[]{:S(2)}) collective-permute-start(f32[128,2048]{1,0:T(8,128)} %get-tuple-element.82), channel_id=1, source_target_pairs={{0,4},{4,8},{8,12},{12,16},{16,20},{20,24},{24,28},{1,5},{5,9},{9,... | collective-permute-start | bytes 3145736 | tf_op jit(solution)/shard_map/ppermute | solution.py:19
  12.0 25.5 %collective-permute-start.1 = (f32[128,2048]{1,0:T(8,128)}, f32[128,2048]{1,0:T(8,128)S(1)}, u32[]{:S(2)}, u32[]{:S(2)}) collective-permute-start(f32[128,2048]{1,0:T(8,128)} %get-tuple-element.81), channel_id=1, source_target_pairs={{4,0},{8,4},{12,8},{16,12},{20,16},{24,20},{28,24},{5,1},{9,5},{13... | collective-permute-start | bytes 3145736 | tf_op jit(solution)/shard_map/ppermute | solution.py:21
  22.8 25.8 %slice-start = ((s8[8388608]{0:T(1024)(128)(4,1)}), s8[4194304]{0:T(1024)(128)(4,1)S(1)}, s32[]{:S(2)}) async-start(s8[8388608]{0:T(1024)(128)(4,1)} %bitcast.137), calls=%async_computation.2 | async-start | bytes 8388608
  24.2 24.3 %slice-start.1 = ((s8[8388608]{0:T(1024)(128)(4,1)}), s8[4194304]{0:T(1024)(128)(4,1)S(1)}, s32[]{:S(2)}) async-start(s8[8388608]{0:T(1024)(128)(4,1)} %bitcast.137), calls=%async_computation.3 | async-start | bytes 8388608
  37.5 11.0 %copy-start.3 = (f32[128,2048]{1,0:T(8,128)}, f32[128,2048]{1,0:T(8,128)S(1)}, u32[]{:S(2)}) copy-start(f32[128,2048]{1,0:T(8,128)S(1)} %collective-permute-done.1) | copy-start | bytes 3145732
  72.6 33.2 %collective-permute-start.2 = (f32[128,2048]{1,0:T(8,128)}, f32[128,2048]{1,0:T(8,128)}, u32[]{:S(2)}, u32[]{:S(2)}) collective-permute-start(f32[128,2048]{1,0:T(8,128)} %get-tuple-element.74), channel_id=1, source_target_pairs={{0,4},{4,8},{8,12},{12,16},{16,20},{20,24},{24,28},{1,5},{5,9},{9,... | collective-permute-start | bytes 3145736 | tf_op jit(solution)/shard_map/ppermute | solution.py:19
  78.7 27.1 %collective-permute-start.3 = (f32[128,2048]{1,0:T(8,128)}, f32[128,2048]{1,0:T(8,128)}, u32[]{:S(2)}, u32[]{:S(2)}) collective-permute-start(f32[128,2048]{1,0:T(8,128)} %get-tuple-element.73), channel_id=1, source_target_pairs={{4,0},{8,4},{12,8},{16,12},{20,16},{24,20},{28,24},{5,1},{9,5},{13... | collective-permute-start | bytes 3145736 | tf_op jit(solution)/shard_map/ppermute | solution.py:21
  80.0 36.6 %slice-start.2 = ((s8[8388608]{0:T(1024)(128)(4,1)}), s8[4194304]{0:T(1024)(128)(4,1)S(1)}, s32[]{:S(2)}) async-start(s8[8388608]{0:T(1024)(128)(4,1)} %bitcast.140), calls=%async_computation.4 | async-start | bytes 8388608
  92.7 23.9 %slice-start.3 = ((s8[8388608]{0:T(1024)(128)(4,1)}), s8[4194304]{0:T(1024)(128)(4,1)S(1)}, s32[]{:S(2)}) async-start(s8[8388608]{0:T(1024)(128)(4,1)} %bitcast.140), calls=%async_computation.5 | async-start | bytes 8388608
  140.0 30.1 %collective-permute-start.4 = (f32[128,2048]{1,0:T(8,128)}, f32[128,2048]{1,0:T(8,128)S(1)}, u32[]{:S(2)}, u32[]{:S(2)}) collective-permute-start(f32[128,2048]{1,0:T(8,128)} %get-tuple-element.65), channel_id=1, source_target_pairs={{0,4},{4,8},{8,12},{12,16},{16,20},{20,24},{24,28},{1,5},{5,9},{9,... | collective-permute-start | bytes 3145736 | tf_op jit(solution)/shard_map/ppermute | solution.py:19
  143.3 26.7 %collective-permute-start.5 = (f32[128,2048]{1,0:T(8,128)}, f32[128,2048]{1,0:T(8,128)}, u32[]{:S(2)}, u32[]{:S(2)}) collective-permute-start(f32[128,2048]{1,0:T(8,128)} %get-tuple-element.66), channel_id=1, source_target_pairs={{4,0},{8,4},{12,8},{16,12},{20,16},{24,20},{28,24},{5,1},{9,5},{13... | collective-permute-start | bytes 3145736 | tf_op jit(solution)/shard_map/ppermute | solution.py:21
  144.9 12.5 %slice-start.4 = ((s8[8388608]{0:T(1024)(128)(4,1)}), s8[4194304]{0:T(1024)(128)(4,1)S(1)}, s32[]{:S(2)}) async-start(s8[8388608]{0:T(1024)(128)(4,1)} %bitcast.142), calls=%async_computation.6 | async-start | bytes 8388608
  185.0 36.8 %collective-permute-start.6 = (f32[1024,384]{1,0:T(8,128)S(1)}, f32[1024,384]{1,0:T(8,128)S(1)}, u32[]{:S(2)}, u32[]{:S(2)}) collective-permute-start(f32[1024,384]{1,0:T(8,128)S(1)} %get-tuple-element.59), channel_id=1, source_target_pairs={{0,1},{1,2},{2,3},{4,5},{5,6},{6,7},{8,9},{9,10},{10,11},{12,13},{... | collective-permute-start | bytes 4718600 | tf_op jit(solution)/shard_map/ppermute | solution.py:19
  188.5 68.9 %collective-permute-start.7 = (f32[1024,384]{1,0:T(8,128)S(1)}, f32[1024,384]{1,0:T(8,128)S(1)}, u32[]{:S(2)}, u32[]{:S(2)}) collective-permute-start(f32[1024,384]{1,0:T(8,128)S(1)} %get-tuple-element.60), channel_id=1, source_target_pairs={{1,0},{2,1},{3,2},{5,4},{6,5},{7,6},{9,8},{10,9},{11,10},{13,12},{... | collective-permute-start | bytes 4718600 | tf_op jit(solution)/shard_map/ppermute | solution.py:21
  274.0 20.1 %copy-start = (f32[1024,2816]{0,1:T(8,128)S(1)}, f32[1024,2816]{0,1:T(8,128)}, u32[]{:S(2)}) copy-start(f32[1024,2816]{0,1:T(8,128)} %copy.32) | copy-start | bytes 34603012
  328.3 10.8 %copy-start.1 = (f32[1024,18,128]{0,2,1:T(8,128)S(1)}, f32[1024,18,128]{0,2,1:T(8,128)}, u32[]{:S(2)}) copy-start(f32[1024,18,128]{0,2,1:T(8,128)} %fusion.10) | copy-start | bytes 28311556
  328.3 10.9 %copy-start.6 = (pred[16,128]{1,0:T(8,128)(4,1)S(1)}, pred[16,128]{1,0:T(8,128)(4,1)}, u32[]{:S(2)}) copy-start(pred[16,128]{1,0:T(8,128)(4,1)} %fusion.58) | copy-start | bytes 6148
  328.3 10.9 %copy-start.7 = (pred[16,128]{1,0:T(8,128)(4,1)S(1)}, pred[16,128]{1,0:T(8,128)(4,1)}, u32[]{:S(2)}) copy-start(pred[16,128]{1,0:T(8,128)(4,1)} %fusion.59) | copy-start | bytes 6148
  328.3 10.9 %copy-start.14 = (f32[16]{0:T(128)S(1)}, f32[16]{0:T(128)}, u32[]{:S(2)}) copy-start(f32[16]{0:T(128)} %slice_bitcast_fusion.16) | copy-start | bytes 196
  354.9 126.0 %all-reduce.11.cloned.1.call-start = ((), (), s32[]{:S(2)}) async-start(), calls=%async_computation.1 | async-start | bytes 4718592 | tf_op jit(solution)/shard_map/psum | solution.py:109
  370.0 110.9 %copy-start.10 = (f32[256]{0:T(256)S(1)}, f32[256]{0:T(256)}, u32[]{:S(2)}) copy-start(f32[256]{0:T(256)} %param.13) | copy-start | bytes 3076
  480.9 67.0 %copy-start.4 = (f32[256,2048]{1,0:T(8,128)S(1)}, f32[256,2048]{1,0:T(8,128)}, u32[]{:S(2)}) copy-start(f32[256,2048]{1,0:T(8,128)} %get-tuple-element.33) | copy-start | bytes 6291460
  520.0 33.1 %copy-start.2 = (f32[1024,256]{0,1:T(8,128)S(1)}, f32[1024,256]{0,1:T(8,128)}, u32[]{:S(2)}) copy-start(f32[1024,256]{0,1:T(8,128)} %all-reduce.9.cloned.1.call-done) | copy-start | bytes 3145732
  (8 other events, 51.5 us)
Sparse Core Ops, SparseCore 0:
  355.0 55.2 all-reduce.8
  413.8 66.9 all-reduce.10
where the time goes:
time: 581 us; the launch traced here: 572 us
  other arithmetic  217 us (37%)
  waiting for transfers between devices  173 us (30%)
  local copies, waits for them, and re-layouts  126 us (22%)
  starting transfers between devices  21.2 us (4%)
  matrix products  19.4 us (3%)
  between operations  15.6 us (3%)
    sub x5, other arithmetic, advect(): return q - cu * (q - lon_up) - cv * (q - lat_up)  77.2 us
    slice x10, local copies, waits for them, and re-layouts, advect(): jnp.roll(q, -1, lat_axis + 1)  67.9 us
    psum x1, waiting for transfers between devices, shards(): measured_background_lines, hpht = lax.psum((hp_local, inner_local), 'row')  67.1 us
    psum x1, waiting for transfers between devices, shards(): background_product_gain = lax.psum(pht_local, 'col')  38.6 us
    mul x3, other arithmetic, shards(): advect(current[:, 1:-1], current[:, :-2], current[:, 2:], col_cu[:, low:h...  35.7 us
    ppermute x4, waiting for transfers between devices, padded_2(): lax.ppermute(head, axis, [((i + 1) % count, i) for i in range(ends)])  35.7 us
    another operation x7, other arithmetic, shards(): factor = jnp.linalg.cholesky(innovation)  34.7 us
    ppermute x4, waiting for transfers between devices, padded_2(): lax.ppermute(tail, axis, [(i, (i + 1) % count) for i in range(ends)])  31.5 us
  transfers between devices with their start and end apart: 10, of which 4 were waited for; matrix products, arithmetic and copies ran while one was open for 16% of the time, Pallas kernels for 0%

commit v1 on v0

v1 whole, which is shorter than its diff:
```python
import functools

import jax
import jax.numpy as jnp
from jax import lax
from jax.experimental import pallas as pl
from jax.experimental.pallas import tpu as pltpu
from jax.sharding import PartitionSpec as P

LON = 128
STEPS = 3
MARGIN = STEPS * LON
VMEM_LIMIT = 48 * 1024 * 1024
HIGHEST = lax.Precision.HIGHEST
HIGH = lax.Precision.HIGH


def params():
    return pltpu.CompilerParams(vmem_limit_bytes=VMEM_LIMIT)


def halos(x, axis, dim):
    count = lax.axis_size(axis)
    size = x.shape[dim]
    before, after = [], []
    left, hop = MARGIN, 1
    while left > 0:
        take = min(left, size)
        tail = lax.slice_in_dim(x, size - take, size, axis=dim)
        head = lax.slice_in_dim(x, 0, take, axis=dim)
        before.insert(0, lax.ppermute(tail, axis, [(i, i + hop) for i in range(count - hop)]))
        after.append(lax.ppermute(head, axis, [(i + hop, i) for i in range(count - hop)]))
        left, hop = left - take, hop + 1
    if len(before) == 1:
        return before[0], after[0]
    return jnp.concatenate(before, axis=dim), jnp.concatenate(after, axis=dim)


def advance(q, minus, plus, cu, cv, su, sv, dim):
    lon = jnp.where(su > 0, pltpu.roll(q, 1, dim), pltpu.roll(q, LON - 1, dim))
    lat = jnp.where(sv > 0, minus, plus)
    return q - cu * (q - lon) - cv * (q - lat)


def row_kernel(bands, x, lo, hi, cu, cv, su, sv, out, buf):
    total = bands + 2 * STEPS

    def raw(k):
        if k < STEPS:
            return lo[k * LON : (k + 1) * LON, :]
        if k < STEPS + bands:
            return x[(k - STEPS) * LON : (k - STEPS + 1) * LON, :]
        k -= STEPS + bands
        return hi[k * LON : (k + 1) * LON, :]

    get = raw
    for s in range(STEPS):
        for k in range(s + 1, total - 1 - s):
            r = slice(k * LON, (k + 1) * LON)
            new = advance(get(k), get(k - 1), get(k + 1), cu[r], cv[r], su[r], sv[r], 0)
            if s == STEPS - 1:
                out[(k - STEPS) * LON : (k - STEPS + 1) * LON, :] = new
            else:
                buf[s, r, :] = new
        get = lambda k, s=s: buf[s, k * LON : (k + 1) * LON, :]


def row_transport(x, lo, hi, coeffs, tiles, column_of):
    rows = x.shape[0]
    wide = rows + 2 * MARGIN
    const = pl.BlockSpec((wide, LON), lambda j: (0, 0))
    return pl.pallas_call(
        functools.partial(row_kernel, rows // LON),
        grid=(tiles,),
        in_specs=[
            pl.BlockSpec((rows, LON), lambda j: (0, column_of(j))),
            pl.BlockSpec((MARGIN, LON), lambda j: (0, j)),
            pl.BlockSpec((MARGIN, LON), lambda j: (0, j)),
            const,
            const,
            const,
            const,
        ],
        out_specs=pl.BlockSpec((rows, LON), lambda j: (0, j)),
        out_shape=jax.ShapeDtypeStruct((rows, tiles * LON), jnp.float32),
        scratch_shapes=[pltpu.VMEM((2, wide, LON), jnp.float32)],
        compiler_params=params(),
        cost_estimate=pl.CostEstimate(
            flops=30 * wide * tiles * LON, bytes_accessed=8 * wide * tiles * LON, transcendentals=0
        ),
    )(x, lo, hi, *coeffs)


def col_steps(raw, total, cu, cv, su, sv, buf, finish):
    get = raw
    for s in range(STEPS):
        for k in range(s + 1, total - 1 - s):
            c = slice(k * LON, (k + 1) * LON)
            new = advance(get(k), get(k - 1), get(k + 1), cu[:, c], cv[:, c], su[:, c], sv[:, c], 1)
            if s == STEPS - 1:
                finish(k - STEPS, new)
            else:
                buf[s, :, c] = new
        get = lambda k, s=s: buf[s, :, k * LON : (k + 1) * LON]


def band_reader(pieces):
    table = [(ref, first + k) for ref, first, n in pieces for k in range(n)]

    def raw(k):
        ref, at = table[k]
        return ref[:, at * LON : (at + 1) * LON]

    return raw, len(table)


def final_kernel(pieces, n, *args):
    refs, (pht, w, cu, cv, su, sv, out, buf) = args[:n], args[n:]
    raw, total = band_reader([(refs[i], f, c) for i, f, c in pieces])
    gain = pht[...]

    def finish(k, new):
        c = slice(k * LON, (k + 1) * LON)
        out[:, c] = new - out[:, c]

    for c in range(0, out.shape[1], 512):
        d = slice(c, min(c + 512, out.shape[1]))
        out[:, d] = jnp.dot(gain, w[:, d], precision=HIGHEST, preferred_element_type=jnp.float32)
    col_steps(raw, total, cu, cv, su, sv, buf, finish)


def weights_kernel(a, lo, hi, inv, cu, cv, su, sv, w, hp, buf):
    bands = a.shape[1] // LON
    raw, total = band_reader([(lo, 0, STEPS), (a, 0, bands), (hi, 0, STEPS)])

    def finish(k, new):
        hp[:, k * LON : (k + 1) * LON] = new

    col_steps(raw, total, cu, cv, su, sv, buf, finish)
    for c in range(0, w.shape[1], 512):
        d = slice(c, min(c + 512, w.shape[1]))
        w[:, d] = jnp.dot(inv[...], hp[:, d], precision=HIGHEST, preferred_element_type=jnp.float32)


def site_kernel(start_ref, site, cu, cv, su, sv, out):
    total = cu.shape[1] // LON
    rows = site.shape[0]
    where = jnp.broadcast_to(site[...] - start_ref[0] + MARGIN, (rows, LON))
    lane = lax.broadcasted_iota(jnp.int32, (rows, LON), 1)
    v = [jnp.where(where == lane + k * LON, 1.0, 0.0) for k in range(total)]
    for s in range(STEPS):
        lo, hi = s + 1, total - 1 - s
        down, up, new = {}, {}, []
        for k in range(lo - 1, hi + 1):
            c = slice(k * LON, (k + 1) * LON)
            t = cv[:, c] * v[k]
            down[k] = jnp.where(sv[:, c] > 0, t, 0.0)
            up[k] = jnp.where(sv[:, c] > 0, 0.0, t)
        for k in range(total):
            if k < lo or k >= hi:
                new.append(v[k])
                continue
            c = slice(k * LON, (k + 1) * LON)
            t = cu[:, c] * v[k]
            west = pltpu.roll(jnp.where(su[:, c] > 0, t, 0.0), LON - 1, 1)
            east = pltpu.roll(jnp.where(su[:, c] > 0, 0.0, t), 1, 1)
            keep = v[k] - t - cv[:, c] * v[k]
            new.append(keep + west + east + down[k + 1] + up[k - 1])
        v = new
    for k in range(STEPS, total - STEPS):
        out[:, (k - STEPS) * LON : (k - STEPS + 1) * LON] = v[k]


def site_rows(site, start, coeffs):
    wide = coeffs[0].shape[1]
    nobs = site.shape[0]
    tile = 8
    const = pl.BlockSpec((1, wide), lambda i, s: (0, 0))
    return pl.pallas_call(
        site_kernel,
        grid_spec=pltpu.PrefetchScalarGridSpec(
            num_scalar_prefetch=1,
            grid=(nobs // tile,),
            in_specs=[pl.BlockSpec((tile, 1), lambda i, s: (i, 0)), const, const, const, const],
            out_specs=pl.BlockSpec((tile, wide - 2 * MARGIN), lambda i, s: (i, 0)),
        ),
        out_shape=jax.ShapeDtypeStruct((nobs, wide - 2 * MARGIN), jnp.float32),
        compiler_params=params(),
    )(start.reshape(1).astype(jnp.int32), site.reshape(nobs, 1), *coeffs)


def sweep_inverse(a):
    n = a.shape[0]
    sub = lax.broadcasted_iota(jnp.int32, (n, n), 0)
    lane = lax.broadcasted_iota(jnp.int32, (n, n), 1)

    def body(_, a):
        for i in range(8):
            r = 1.0 / a[i : i + 1, i : i + 1]
            row = a[i : i + 1, :] * r
            col = a[:, i : i + 1]
            new = jnp.where(lane == i, col * r, a - col * row)
            a = jnp.where(sub == i, jnp.where(lane == i, -r, row), new)
        a = jnp.concatenate([a[8:], a[:8]], axis=0)
        return pltpu.roll(a, n - 8, 1)

    return -lax.fori_loop(0, n // 8, body, a)


def mm(x, y):
    return jnp.dot(x, y, precision=HIGHEST, preferred_element_type=jnp.float32)


def inverse(a):
    n = a.shape[0]
    if n <= LON:
        return sweep_inverse(a)
    h = n // 2
    s12, s22 = a[:h, h:], a[h:, h:]
    i1 = inverse(a[:h, :h])
    x = mm(i1, s12)
    i2 = inverse(s22 - mm(s12.T, x))
    y = mm(x, i2)
    return jnp.concatenate(
        [
            jnp.concatenate([i1 + mm(y, x.T), -y], axis=1),
            jnp.concatenate([-y.T, i2], axis=1),
        ],
        axis=0,
    )


def inverse_kernel(s, r, out):
    n = s.shape[0]
    sub = lax.broadcasted_iota(jnp.int32, (n, n), 0)
    lane = lax.broadcasted_iota(jnp.int32, (n, n), 1)
    a = s[...] + jnp.where(sub == lane, jnp.broadcast_to(r[...], (n, n)), 0.0)
    out[...] = inverse(0.5 * (a + a.T))


def shards(
    covariance, lon_speed, lat_speed, lon_sign, lat_sign, measurement_site_position, obs_var
):
    rows, cols = covariance.shape
    nobs = obs_var.shape[0]
    row_start = lax.axis_index("row") * rows
    col_start = lax.axis_index("col") * cols
    fields = jnp.stack(
        [lon_speed, lat_speed, lon_sign.astype(jnp.float32), lat_sign.astype(jnp.float32)]
    )
    fields = jnp.pad(fields, ((0, 0), (MARGIN, MARGIN)))
    row_fields = lax.dynamic_slice_in_dim(fields, row_start, rows + 2 * MARGIN, axis=1)
    col_fields = lax.dynamic_slice_in_dim(fields, col_start, cols + 2 * MARGIN, axis=1)
    row_lines = [row_fields[i : i + 1] for i in range(4)]
    col_lines = [col_fields[i : i + 1] for i in range(4)]
    row_coeffs = [
        jnp.broadcast_to(row_fields[i][:, None], (rows + 2 * MARGIN, LON)) for i in range(4)
    ]

    tiles = cols // LON
    split = tiles > 2 * STEPS
    if split:
        edge_cols = jnp.concatenate([covariance[:, :MARGIN], covariance[:, cols - MARGIN :]], axis=1) if rows < MARGIN else None
        if edge_cols is None:
            head = jnp.concatenate([covariance[:MARGIN, :MARGIN], covariance[:MARGIN, cols - MARGIN :]], axis=1)
            tail = jnp.concatenate(
                [covariance[rows - MARGIN :, :MARGIN], covariance[rows - MARGIN :, cols - MARGIN :]], axis=1
            )
            count = lax.axis_size("row")
            edge_lo = lax.ppermute(tail, "row", [(i, i + 1) for i in range(count - 1)])
            edge_hi = lax.ppermute(head, "row", [(i + 1, i) for i in range(count - 1)])
        else:
            edge_lo, edge_hi = halos(edge_cols, "row", 0)
        mid_lo, mid_hi = halos(covariance[:, MARGIN : cols - MARGIN], "row", 0)
        skip = tiles - 2 * STEPS
        edges = row_transport(
            covariance, edge_lo, edge_hi, row_coeffs, 2 * STEPS,
            lambda j: jnp.where(j < STEPS, j, j + skip),
        )
        first, last = edges[:, :MARGIN], edges[:, MARGIN:]
        count = lax.axis_size("col")
        left = lax.ppermute(last, "col", [(i, i + 1) for i in range(count - 1)])
        right = lax.ppermute(first, "col", [(i + 1, i) for i in range(count - 1)])
        middle = row_transport(
            covariance, mid_lo, mid_hi, row_coeffs, skip, lambda j: j + STEPS
        )
        arrays = [left, edges, middle, right]
        pieces = [(0, 0, STEPS), (1, 0, STEPS), (2, 0, skip), (1, STEPS, STEPS), (3, 0, STEPS)]
    else:
        lo, hi = halos(covariance, "row", 0)
        whole = row_transport(covariance, lo, hi, row_coeffs, tiles, lambda j: j)
        left, right = halos(whole, "col", 1)
        arrays = [left, whole, right]
        pieces = [(0, 0, STEPS), (1, 0, tiles), (2, 0, STEPS)]

    g_row = site_rows(measurement_site_position, row_start, row_lines)
    g_col = site_rows(measurement_site_position, col_start, col_lines)
    dot = functools.partial(
        lax.dot_general, precision=HIGH, preferred_element_type=jnp.float32
    )
    a_part = dot(g_row, covariance, (((1,), (0,)), ((), ())))
    b_part = dot(covariance, g_col, (((1,), (1,)), ((), ())))
    s_part = lax.dot_general(
        a_part, g_col, (((1,), (1,)), ((), ())), precision=HIGHEST, preferred_element_type=jnp.float32
    )
    s = lax.psum(s_part, ("row", "col"))
    a = lax.psum(a_part, "row")
    b = lax.psum(b_part, "col")
    inv = pl.pallas_call(
        inverse_kernel,
        out_shape=jax.ShapeDtypeStruct((nobs, nobs), jnp.float32),
        compiler_params=params(),
    )(s, obs_var.reshape(1, nobs))
    b_lo, b_hi = halos(b, "row", 0)
    pht = row_transport(b, b_lo, b_hi, row_coeffs, nobs // LON, lambda j: j)
    a_lo, a_hi = halos(a, "col", 1)
    wide = cols + 2 * MARGIN
    w = pl.pallas_call(
        weights_kernel,
        out_shape=jax.ShapeDtypeStruct((nobs, cols), jnp.float32),
        scratch_shapes=[
            pltpu.VMEM((nobs, cols), jnp.float32),
            pltpu.VMEM((2, nobs, wide), jnp.float32),
        ],
        compiler_params=params(),
    )(a, a_lo, a_hi, inv, *col_lines)

    tile = LON
    return pl.pallas_call(
        functools.partial(final_kernel, pieces, len(arrays)),
        grid=(rows // tile,),
        in_specs=[pl.BlockSpec((tile, x.shape[1]), lambda i: (i, 0)) for x in arrays]
        + [
            pl.BlockSpec((tile, nobs), lambda i: (i, 0)),
            pl.BlockSpec((nobs, cols), lambda i: (0, 0)),
        ]
        + [pl.BlockSpec((1, wide), lambda i: (0, 0))] * 4,
        out_specs=pl.BlockSpec((tile, cols), lambda i: (i, 0)),
        out_shape=jax.ShapeDtypeStruct((rows, cols), jnp.float32),
        scratch_shapes=[pltpu.VMEM((2, tile, wide), jnp.float32)],
        compiler_params=params(),
    )(*arrays, pht, w, *col_lines)


def solution(mesh):
    return jax.shard_map(
        shards,
        mesh=mesh,
        in_specs=(P("row", "col"), P(), P(), P(), P(), P(), P()),
        out_specs=P("row", "col"),
        check_vma=False,
    )
```

time: 581 us -> 467 us (0.80); the launches traced: 572 us -> 466 us
  other arithmetic: 217 us -> 4.66 us
  Pallas kernels: 0 us -> 111 us
  local copies, waits for them, and re-layouts: 126 us -> 24.8 us
  waiting for transfers between devices: 173 us -> 261 us
  starting transfers between devices: 21.2 us -> 34.6 us
    psum x2 -> x3, waiting for transfers between devices: 106 us -> 253 us  [the longest x1 156 us: shards(): s = lax.psum(s_part, ('row', 'col'))]
    pallas_call x0 -> x8, Pallas kernels: none -> 111 us  [the longest x1 32 us: shards(): pl.pallas_call(inverse_kernel, out_shape=jax.ShapeDtypeStruct((nobs, nobs...]
    sub x5 -> x0, other arithmetic: 77.2 us -> none  [advect(): return q - cu * (q - lon_up) - cv * (q - lat_up)]
    slice x16 -> x7, local copies, waits for them, and re-layouts: 80.1 us -> 14.1 us  [the longest x3 8.14 us: halos(): head = lax.slice_in_dim(x, 0, take, axis=dim)]
    ppermute x8 -> x10, waiting for transfers between devices: 67.2 us -> 7.67 us  [the longest x3 5.33 us: halos(): lax.ppermute(tail, axis, [(i, i + hop) for i in range(count - hop)])]
    another operation x10 -> x1, other arithmetic: 55.3 us -> 0.9 us  [shards(): jnp.stack([lon_speed, lat_speed, lon_sign.astype(jnp.float32), lat_sign.a...]
    concatenate x5 -> x2, other arithmetic: 38.8 us -> 2.23 us  [the longest x1 1.13 us: shards(): jnp.concatenate([covariance[rows - MARGIN:, :MARGIN], covariance[rows - M...]
    mul x3 -> x0, other arithmetic: 35.7 us -> none  [shards(): advect(current[:, 1:-1], current[:, :-2], current[:, 2:], col_cu[:, low:h...]
  transfers between devices with their start and end apart: 10 -> 13, of which waited for: 4 -> 5; matrix products, arithmetic and copies ran while one was open for 16% -> 5% of each run, Pallas kernels for 0% -> 13%
where the time goes in v1:
time: 467 us; the launch traced here: 466 us
  waiting for transfers between devices  261 us (56%)
  Pallas kernels  111 us (24%)
  starting transfers between devices  34.6 us (7%)
  local copies, waits for them, and re-layouts  24.8 us (5%)
  between operations  15.2 us (3%)
  matrix products  14.8 us (3%)
    psum x1, waiting for transfers between devices, shards(): s = lax.psum(s_part, ('row', 'col'))  156 us
    psum x1, waiting for transfers between devices, shards(): a = lax.psum(a_part, 'row')  56.6 us
    psum x1, waiting for transfers between devices, shards(): b = lax.psum(b_part, 'col')  40.2 us
    pallas_call x1, Pallas kernels, shards(): pl.pallas_call(inverse_kernel, out_shape=jax.ShapeDtypeStruct((nobs, nobs...  32 us
    pallas_call x3, Pallas kernels, row_transport(): pl.pallas_call(functools.partial(row_kernel, rows // LON), grid=(tiles,),...  25.8 us
    pallas_call x1, Pallas kernels, shards(): pl.pallas_call(functools.partial(final_kernel, pieces, len(arrays)), grid...  25.4 us
    pallas_call x2, Pallas kernels, site_rows(): pl.pallas_call(site_kernel, grid_spec=pltpu.PrefetchScalarGridSpec(num_sc...  22.7 us
    ppermute x3, starting transfers between devices, halos(): lax.ppermute(tail, axis, [(i, i + hop) for i in range(count - hop)])  19 us
  transfers between devices with their start and end apart: 13, of which 5 were waited for; matrix products, arithmetic and copies ran while one was open for 5% of the time, Pallas kernels for 13%

profile of v1, /device:TPU:0, one launch (start us, length us, event | category | flops | bytes accessed | tf_op | source)
XLA Modules:
  0.0 466.1 jit_solution(7360856191263487425)
XLA Ops:
  10.9 10.5 %shard_map.77 = f32[256,1024]{1,0:T(8,128)S(1)} custom-call(s32[1]{0:T(128)} %bitcast.7.start_ref, s32[256,1]{1,0:T(8,128)S(1)} %copy.9.site, f32[1,1792]{1,0:T(1,128)S(1)} %get-tuple-element.34.cu, f32[1,1792]{1,0:T(1,128)S(1)} %get-tuple-element.32.cv, f32[1,1792]{1,0:T(1,128)S(1)} %get-tuple-element.30.su, f32[1,1792]{1,0:T(1,128)S(1)} %get-tuple-element.6.sv), custom_call_target="tpu_custom_call" | custom-call | tf_op jit(solution)/shard_map/pallas_call | solution.py:179
  21.4 7.6 %fusion.11 = f32[256,2048]{1,0:T(8,128)} fusion(f32[256,1024]{1,0:T(8,128)S(1)} %shard_map.77, f32[1024,2048]{1,0:T(8,128)} %x.5), kind=kOutput, calls=%fused_computation.21 | convolution fusion | flops 3221225472 | bytes 11534336 | tf_op jit(solution)/shard_map/dot_general | solution.py:301
  29.0 12.2 %shard_map.75 = f32[256,2048]{1,0:T(8,128)S(1)} custom-call(s32[1]{0:T(128)} %bitcast.4.start_ref, s32[256,1]{1,0:T(8,128)S(1)} %copy.9.site, f32[1,2816]{1,0:T(1,128)S(1)} %get-tuple-element.28.cu.args_6_, f32[1,2816]{1,0:T(1,128)S(1)} %get-tuple-element.27.cv.args_7_, f32[1,2816]{1,0:T(1,128)S(1)} %get-tuple-element.26.su.args_8_, ...), custom_call_target="tpu_custom_call" | custom-call | tf_op jit(solution)/shard_map/pallas_call | solution.py:179
  41.3 2.6 fusion.12
  47.7 2.4 collective-permute-start
  52.7 4.3 fusion.5
  58.3 7.1 %collective-permute-start.3 = (f32[384,1280]{1,0:T(8,128)}, f32[384,1280]{1,0:T(8,128)}, u32[]{:S(2)}, u32[]{:S(2)}) collective-permute-start(f32[384,1280]{1,0:T(8,128)} %get-tuple-element.14), channel_id=1, source_target_pairs={{0,4},{4,8},{8,12},{12,16},{16,20},{20,24},{24,28},{1,5},{5,9},{9,... | collective-permute-start | bytes 5898248 | tf_op jit(solution)/shard_map/ppermute | solution.py:31
  65.4 4.7 convolution_bitcast_fusion
  70.1 56.6 %all-reduce.7.cloned.1.call-done.a = f32[256,2048]{1,0:T(8,128)} async-done(((f32[256,2048]{1,0:T(8,128)}), f32[256,2048]{1,0:T(8,128)}) %all-reduce.7.cloned.1.call-update) | async-done | bytes 2097168 | tf_op jit(solution)/shard_map/psum | solution.py:307
  126.7 1.9 fusion.8
  132.2 9.0 %shard_map.73.args_1_ = f32[1024,768]{1,0:T(8,128)} custom-call(f32[1024,2048]{1,0:T(8,128)} %x.5, f32[384,768]{1,0:T(8,128)S(1)} %copy-done.5, f32[384,768]{1,0:T(8,128)} %collective-permute-done.1.hi, f32[1792,128]{1,0:T(8,128)S(1)} %broadcast_in_dim.29.cu, f32[1792,128]{1,0:T(8,128)S(1)} %broadcast_in_dim.31.cv, f32[1792,128]{1,0:T(8,128)S(1)} %broadcast_in_dim.33.su, ...), custom_call_target="tpu_custom_call" | custom-call | flops 41287680 | bytes 11010048 | tf_op jit(solution)/shard_map/pallas_call | solution.py:72
  141.2 3.8 fusion.7
  146.4 6.4 %collective-permute-start.2 = (f32[1024,384]{1,0:T(8,128)}, f32[1024,384]{1,0:T(8,128)}, u32[]{:S(2)}, u32[]{:S(2)}) collective-permute-start(f32[1024,384]{1,0:T(8,128)} %get-tuple-element.20), channel_id=1, source_target_pairs={{0,1},{1,2},{2,3},{4,5},{5,6},{6,7},{8,9},{9,10},{10,11},{12,13},{... | collective-permute-start | bytes 4718600 | tf_op jit(solution)/shard_map/ppermute | solution.py:282
  153.6 3.8 collective-permute-start.8
  157.4 40.2 %all-reduce.5.cloned.1.call-done.x = f32[1024,256]{1,0:T(8,128)} async-done(((f32[1024,256]{1,0:T(8,128)}), f32[1024,256]{1,0:T(8,128)}) %all-reduce.5.cloned.1.call-update) | async-done | bytes 1048592 | tf_op jit(solution)/shard_map/psum | solution.py:308
  199.5 5.3 %collective-permute-done.8.lo = f32[256,384]{1,0:T(8,128)S(1)} collective-permute-done((f32[256,384]{1,0:T(8,128)}, f32[256,384]{1,0:T(8,128)S(1)}, u32[]{:S(2)}, u32[]{:S(2)}) %collective-permute-start.8) | collective-permute-done | bytes 393248 | tf_op jit(solution)/shard_map/ppermute | solution.py:31
  206.1 2.3 collective-permute-done.7.hi
  209.2 8.1 %collective-permute-start.6 = (f32[384,256]{1,0:T(8,128)}, f32[384,256]{1,0:T(8,128)}, u32[]{:S(2)}, u32[]{:S(2)}) collective-permute-start(f32[384,256]{1,0:T(8,128)} %get-tuple-element.24), channel_id=1, source_target_pairs={{0,4},{4,8},{8,12},{12,16},{16,20},{20,24},{24,28},{1,5},{5,9},{9,... | collective-permute-start | bytes 1179656 | tf_op jit(solution)/shard_map/ppermute | solution.py:31
  217.3 156.0 %all-reduce.9.cloned.1.call-done.s = f32[256,256]{1,0:T(8,128)} async-done(((f32[256,256]{1,0:T(8,128)}), f32[256,256]{1,0:T(8,128)}) %all-reduce.9.cloned.1.call-update) | async-done | bytes 262160 | tf_op jit(solution)/shard_map/psum | solution.py:306
  374.3 32.0 %shard_map.78.inv = f32[256,256]{1,0:T(8,128)S(1)} custom-call(f32[256,256]{1,0:T(8,128)S(1)} %copy-done.10, f32[1,256]{1,0:T(1,128)S(1)} %bitcast.16), custom_call_target="tpu_custom_call" | custom-call | tf_op jit(solution)/shard_map/pallas_call | solution.py:309
  410.0 5.0 %shard_map.79.args_5_ = f32[256,2048]{1,0:T(8,128)S(1)} custom-call(f32[256,2048]{1,0:T(8,128)S(1)} %copy-done.3, f32[256,384]{1,0:T(8,128)S(1)} %collective-permute-done.8.lo, f32[256,384]{1,0:T(8,128)S(1)} %copy-done.7, f32[256,256]{1,0:T(8,128)S(1)} %shard_map.78.inv, f32[1,2816]{1,0:T(1,128)S(1)} %copy-done.18, f32[1,2816]{1,0:T(1,128)S(1)} %copy-done.15, ...), custom_call_target="tpu_custom_call" | custom-call | tf_op jit(solution)/shard_map/pallas_call | solution.py:318
  416.4 3.2 shard_map.76.args_4_
  419.6 13.6 %shard_map.74.args_2_ = f32[1024,1280]{1,0:T(8,128)} custom-call(f32[1024,2048]{1,0:T(8,128)} %x.5, f32[384,1280]{1,0:T(8,128)} %collective-permute-done.3.lo, f32[384,1280]{1,0:T(8,128)} %collective-permute-done.4.hi, f32[1792,128]{1,0:T(8,128)S(1)} %copy-done.1, f32[1792,128]{1,0:T(8,128)S(1)} %broadcast_in_dim.31.cv, ...), custom_call_target="tpu_custom_call" | custom-call | flops 68812800 | bytes 18350080 | tf_op jit(solution)/shard_map/pallas_call | solution.py:72
  433.3 25.4 %shard_map.80 = f32[1024,2048]{1,0:T(8,128)} custom-call(f32[1024,384]{1,0:T(8,128)} %collective-permute-done.2.args_0_, f32[1024,768]{1,0:T(8,128)} %shard_map.73.args_1_, f32[1024,1280]{1,0:T(8,128)} %shard_map.74.args_2_, f32[1024,384]{1,0:T(8,128)} %collective-permute-done.5.args_3_, f32[1024,256]{1,0:T(8,128)S(1)} %shard_map.76.args_4_, ...), custom_call_target="tpu_custom_call" | custom-call | tf_op jit(solution)/shard_map/pallas_call | solution.py:329
  (82 shorter events, 27.0 us)
Async XLA Ops:
  10.0 19.0 %copy-start.11 = (f32[1,2816]{1,0:T(1,128)}, f32[1,2816]{1,0:T(1,128)S(1)}, u32[]{:S(2)}) copy-start(f32[1,2816]{1,0:T(1,128)S(1)} %get-tuple-element.26.su.args_8_) | copy-start | bytes 33796
  10.0 19.0 %copy-start.14 = (f32[1,2816]{1,0:T(1,128)}, f32[1,2816]{1,0:T(1,128)S(1)}, u32[]{:S(2)}) copy-start(f32[1,2816]{1,0:T(1,128)S(1)} %get-tuple-element.27.cv.args_7_) | copy-start | bytes 33796
  10.0 19.0 %copy-start.17 = (f32[1,2816]{1,0:T(1,128)}, f32[1,2816]{1,0:T(1,128)S(1)}, u32[]{:S(2)}) copy-start(f32[1,2816]{1,0:T(1,128)S(1)} %get-tuple-element.28.cu.args_6_) | copy-start | bytes 33796
  29.0 12.3 %copy-start.21 = (f32[256,2048]{1,0:T(8,128)S(1)}, f32[256,2048]{1,0:T(8,128)}, u32[]{:S(2)}) copy-start(f32[256,2048]{1,0:T(8,128)} %fusion.11) | copy-start | bytes 6291460
  43.9 82.9 %all-reduce.7.cloned.1.call-start = ((), (), s32[]{:S(2)}) async-start(), calls=%async_computation.1 | async-start | bytes 4194304 | tf_op jit(solution)/shard_map/psum | solution.py:307
  44.6 153.0 %all-reduce.5.cloned.1.call-start = ((), (), s32[]{:S(2)}) async-start(), calls=%async_computation | async-start | bytes 2097152 | tf_op jit(solution)/shard_map/psum | solution.py:308
  44.6 20.7 %slice-start = ((s8[8388608]{0:T(1024)(128)(4,1)}), s8[4194304]{0:T(1024)(128)(4,1)S(1)}, s32[]{:S(2)}) async-start(s8[8388608]{0:T(1024)(128)(4,1)} %bitcast.17), calls=%async_computation.3 | async-start | bytes 8388608
  47.7 82.2 %collective-permute-start = (f32[384,768]{1,0:T(8,128)}, f32[384,768]{1,0:T(8,128)S(1)}, u32[]{:S(2)}, u32[]{:S(2)}) collective-permute-start(f32[384,768]{1,0:T(8,128)} %pad_maximum_fusion), channel_id=1, source_target_pairs={{0,4},{4,8},{8,12},{12,16},{16,20},{20,24},{24,28},{1,5},{5,9},{9,... | collective-permute-start | bytes 3538952 | tf_op jit(solution)/shard_map/ppermute | solution.py:270
  50.1 15.2 %slice-start.1 = ((s8[8388608]{0:T(1024)(128)(4,1)}), s8[4194304]{0:T(1024)(128)(4,1)S(1)}, s32[]{:S(2)}) async-start(s8[8388608]{0:T(1024)(128)(4,1)} %bitcast.17), calls=%async_computation.4 | async-start | bytes 8388608
  51.2 78.7 %collective-permute-start.1 = (f32[384,768]{1,0:T(8,128)}, f32[384,768]{1,0:T(8,128)}, u32[]{:S(2)}, u32[]{:S(2)}) collective-permute-start(f32[384,768]{1,0:T(8,128)} %pad_maximum_fusion.1), channel_id=1, source_target_pairs={{4,0},{8,4},{12,8},{16,12},{20,16},{24,20},{28,24},{5,1},{9,5},{13... | collective-permute-start | bytes 3538952 | tf_op jit(solution)/shard_map/ppermute | solution.py:271
  57.0 362.7 %collective-permute-start.4 = (f32[384,1280]{1,0:T(8,128)}, f32[384,1280]{1,0:T(8,128)}, u32[]{:S(2)}, u32[]{:S(2)}) collective-permute-start(f32[384,1280]{1,0:T(8,128)} %get-tuple-element.13), channel_id=1, source_target_pairs={{4,0},{8,4},{12,8},{16,12},{20,16},{24,20},{28,24},{5,1},{9,5},{13... | collective-permute-start | bytes 5898248 | tf_op jit(solution)/shard_map/ppermute | solution.py:32
  58.3 361.4 %collective-permute-start.3 = (f32[384,1280]{1,0:T(8,128)}, f32[384,1280]{1,0:T(8,128)}, u32[]{:S(2)}, u32[]{:S(2)}) collective-permute-start(f32[384,1280]{1,0:T(8,128)} %get-tuple-element.14), channel_id=1, source_target_pairs={{0,4},{4,8},{8,12},{12,16},{16,20},{20,24},{24,28},{1,5},{5,9},{9,... | collective-permute-start | bytes 5898248 | tf_op jit(solution)/shard_map/ppermute | solution.py:31
  70.0 303.3 %all-reduce.9.cloned.1.call-start = ((), (), s32[]{:S(2)}) async-start(), calls=%async_computation.2 | async-start | bytes 524288 | tf_op jit(solution)/shard_map/psum | solution.py:306
  128.6 24.2 %collective-permute-start.9 = (f32[256,384]{1,0:T(8,128)S(1)}, f32[256,384]{1,0:T(8,128)S(1)}, u32[]{:S(2)}, u32[]{:S(2)}) collective-permute-start(f32[256,384]{1,0:T(8,128)S(1)} %get-tuple-element.21), channel_id=1, source_target_pairs={{1,0},{2,1},{3,2},{5,4},{6,5},{7,6},{9,8},{10,9},{11,10},{13,12},{... | collective-permute-start | bytes 1179656 | tf_op jit(solution)/shard_map/ppermute | solution.py:32
  141.2 232.1 %copy-start.20 = (f32[256]{0:T(256)S(1)}, f32[256]{0:T(256)}, u32[]{:S(2)}) copy-start(f32[256]{0:T(256)} %param.13) | copy-start | bytes 3076
  145.0 288.3 %collective-permute-start.5 = (f32[1024,384]{1,0:T(8,128)}, f32[1024,384]{1,0:T(8,128)}, u32[]{:S(2)}, u32[]{:S(2)}) collective-permute-start(f32[1024,384]{1,0:T(8,128)} %get-tuple-element.19), channel_id=1, source_target_pairs={{1,0},{2,1},{3,2},{5,4},{6,5},{7,6},{9,8},{10,9},{11,10},{13,12},{... | collective-permute-start | bytes 4718600 | tf_op jit(solution)/shard_map/ppermute | solution.py:283
  146.4 286.8 %collective-permute-start.2 = (f32[1024,384]{1,0:T(8,128)}, f32[1024,384]{1,0:T(8,128)}, u32[]{:S(2)}, u32[]{:S(2)}) collective-permute-start(f32[1024,384]{1,0:T(8,128)} %get-tuple-element.20), channel_id=1, source_target_pairs={{0,1},{1,2},{2,3},{4,5},{5,6},{6,7},{8,9},{9,10},{10,11},{12,13},{... | collective-permute-start | bytes 4718600 | tf_op jit(solution)/shard_map/ppermute | solution.py:282
  153.6 252.7 %copy-start.7 = (f32[256,384]{1,0:T(8,128)S(1)}, f32[256,384]{1,0:T(8,128)}, u32[]{:S(2)}) copy-start(f32[256,384]{1,0:T(8,128)} %copy-done.6) | copy-start | bytes 1179652
  153.6 51.3 %collective-permute-start.8 = (f32[256,384]{1,0:T(8,128)}, f32[256,384]{1,0:T(8,128)S(1)}, u32[]{:S(2)}, u32[]{:S(2)}) collective-permute-start(f32[256,384]{1,0:T(8,128)} %get-tuple-element.22), channel_id=1, source_target_pairs={{0,1},{1,2},{2,3},{4,5},{5,6},{6,7},{8,9},{9,10},{10,11},{12,13},{... | collective-permute-start | bytes 1179656 | tf_op jit(solution)/shard_map/ppermute | solution.py:31
  204.8 3.6 collective-permute-start.7
  209.2 207.2 %collective-permute-start.6 = (f32[384,256]{1,0:T(8,128)}, f32[384,256]{1,0:T(8,128)}, u32[]{:S(2)}, u32[]{:S(2)}) collective-permute-start(f32[384,256]{1,0:T(8,128)} %get-tuple-element.24), channel_id=1, source_target_pairs={{0,4},{4,8},{8,12},{12,16},{16,20},{20,24},{24,28},{1,5},{5,9},{9,... | collective-permute-start | bytes 1179656 | tf_op jit(solution)/shard_map/ppermute | solution.py:31
  419.6 13.7 %copy-start.13 = (f32[1,2816]{1,0:T(1,128)S(1)}, f32[1,2816]{1,0:T(1,128)}, u32[]{:S(2)}) copy-start(f32[1,2816]{1,0:T(1,128)} %copy-done.11) | copy-start | bytes 33796
  419.6 13.7 %copy-start.16 = (f32[1,2816]{1,0:T(1,128)S(1)}, f32[1,2816]{1,0:T(1,128)}, u32[]{:S(2)}) copy-start(f32[1,2816]{1,0:T(1,128)} %copy-done.14) | copy-start | bytes 33796
  419.6 13.7 %copy-start.19 = (f32[1,2816]{1,0:T(1,128)S(1)}, f32[1,2816]{1,0:T(1,128)}, u32[]{:S(2)}) copy-start(f32[1,2816]{1,0:T(1,128)} %copy-done.17) | copy-start | bytes 33796
  (13 other events, 31.7 us)
Sparse Core Ops, SparseCore 0:
  47.0 79.6 all-reduce.6
  129.8 67.7 all-reduce.4
Sparse Core Ops, SparseCore 1:
  217.4 155.9 all-reduce.8

commit v2 on v1

--- a/solution.py
+++ b/solution.py
@@ -174,7 +174,7 @@
 def site_rows(site, start, coeffs):
     wide = coeffs[0].shape[1]
     nobs = site.shape[0]
-    tile = 8
+    tile = min(nobs, 64)
     const = pl.BlockSpec((1, wide), lambda i, s: (0, 0))
     return pl.pallas_call(
         site_kernel,
@@ -236,6 +236,145 @@
     lane = lax.broadcasted_iota(jnp.int32, (n, n), 1)
     a = s[...] + jnp.where(sub == lane, jnp.broadcast_to(r[...], (n, n)), 0.0)
     out[...] = inverse(0.5 * (a + a.T))
+
+
+def partner_of(axis, d):
+    me = lax.axis_index(axis)
+    bit = (me // d) % 2
+    return bit, me + d - 2 * d * bit
+
+
+def exchange(src, dst, axis, peer, sems, i):
+    return pltpu.make_async_remote_copy(
+        src_ref=src,
+        dst_ref=dst,
+        send_sem=sems.at[0, i],
+        recv_sem=sems.at[1, i],
+        device_id={axis: peer},
+        device_id_type=pl.DeviceIdType.MESH,
+    )
+
+
+def powers(count):
+    return [1 << t for t in range(count.bit_length() - 1)]
+
+
+def reduce_scatter(acc, rx, axis, count, sems, base):
+    rows = acc.shape[0]
+    off, size, at = 0, rows, 0
+    for t, d in enumerate(powers(count)):
+        bit, peer = partner_of(axis, d)
+        half = size // 2
+        keep = pl.multiple_of(off + bit * half, 8)
+        give = pl.multiple_of(off + (1 - bit) * half, 8)
+        copy = exchange(
+            acc.at[pl.ds(give, half), :], rx.at[at : at + half, :], axis, peer, sems, base + t
+        )
+        copy.start()
+        yield
+        copy.wait()
+        acc[pl.ds(keep, half), :] += rx[at : at + half, :]
+        off, size, at = keep, half, at + half
+    return off, size
+
+
+def all_gather(out, off, size, axis, count, sems, base):
+    for t, d in enumerate(reversed(powers(count))):
+        bit, peer = partner_of(axis, d)
+        part = out.at[pl.ds(pl.multiple_of(off, 8), size), :]
+        copy = exchange(part, part, axis, peer, sems, base + t)
+        copy.start()
+        yield
+        copy.wait()
+        off, size = off - bit * size, size * 2
+
+
+def all_reduce(acc, rx, out, axis, count, sems, base):
+    off, size = yield from reduce_scatter(acc, rx, axis, count, sems, base)
+    own = pl.ds(pl.multiple_of(off, 8), size)
+    out[own, :] = acc[own, :]
+    yield from all_gather(out, off, size, axis, count, sems, base + len(powers(count)))
+
+
+def butterfly(acc, rx, sizes, sems, base):
+    t = 0
+    for axis, count in sizes:
+        for d in powers(count):
+            _, peer = partner_of(axis, d)
+            copy = exchange(acc.at[t], rx.at[t], axis, peer, sems, base + t)
+            copy.start()
+            yield
+            copy.wait()
+            acc[t + 1] = acc[t] + rx[t]
+            t += 1
+
+
+def sums_kernel(sizes, a, b, s, a_out, b_out, s_out, a_acc, a_rx, a_all, b_acc, b_rx, b_all, s_acc, s_rx, sems):
+    barrier = pltpu.get_barrier_semaphore()
+    greeted = 0
+    for axis, count in sizes:
+        for d in powers(count):
+            _, peer = partner_of(axis, d)
+            pl.semaphore_signal(
+                barrier, inc=1, device_id={axis: peer}, device_id_type=pl.DeviceIdType.MESH
+            )
+            greeted += 1
+    pl.semaphore_wait(barrier, greeted)
+    (row, rows), (col, cols) = sizes
+    nobs = s.shape[0]
+    tiles = a.shape[1] // LON
+    s_acc[0] = s[...]
+    for k in range(tiles):
+        a_acc[k * nobs : (k + 1) * nobs, :] = a[:, k * LON : (k + 1) * LON]
+    b_acc[...] = b[...]
+    n_row, n_col = len(powers(rows)), len(powers(cols))
+    live = [
+        butterfly(s_acc, s_rx, sizes, sems, 0),
+        all_reduce(a_acc, a_rx, a_all, row, rows, sems, n_row + n_col),
+        all_reduce(b_acc, b_rx, b_all, col, cols, sems, 3 * n_row + n_col),
+    ]
+    while live:
+        still = []
+        for run in live:
+            try:
+                next(run)
+                still.append(run)
+            except StopIteration:
+                pass
+        live = still
+    s_out[...] = s_acc[n_row + n_col]
+    b_out[...] = b_all[...]
+    for k in range(tiles):
+        a_out[:, k * LON : (k + 1) * LON] = a_all[k * nobs : (k + 1) * nobs, :]
+
+
+def sums(a, b, s):
+    sizes = [(axis, lax.axis_size(axis)) for axis in ("row", "col")]
+    stages = [len(powers(n)) for _, n in sizes]
+    nobs = s.shape[0]
+    tall = a.shape[0] * a.shape[1] // LON
+    vmem = pl.BlockSpec(memory_space=pltpu.VMEM)
+    f32 = jnp.float32
+    return pl.pallas_call(
+        functools.partial(sums_kernel, sizes),
+        in_specs=[vmem] * 3,
+        out_specs=[vmem] * 3,
+        out_shape=[jax.ShapeDtypeStruct(x.shape, f32) for x in (a, b, s)],
+        scratch_shapes=[
+            pltpu.VMEM((tall, LON), f32),
+            pltpu.VMEM((tall, LON), f32),
+            pltpu.VMEM((tall, LON), f32),
+            pltpu.VMEM(b.shape, f32),
+            pltpu.VMEM(b.shape, f32),
+            pltpu.VMEM(b.shape, f32),
+            pltpu.VMEM((sum(stages) + 1, nobs, nobs), f32),
+            pltpu.VMEM((sum(stages), nobs, nobs), f32),
+            pltpu.SemaphoreType.DMA((2, 3 * sum(stages))),
+        ],
+        compiler_params=pltpu.CompilerParams(
+            collective_id=0, has_side_effects=True, vmem_limit_bytes=VMEM_LIMIT
+        ),
+    )(a, b, s)
 
 
 def shards(
@@ -303,9 +442,7 @@
     s_part = lax.dot_general(
         a_part, g_col, (((1,), (1,)), ((), ())), precision=HIGHEST, preferred_element_type=jnp.float32
     )
-    s = lax.psum(s_part, ("row", "col"))
-    a = lax.psum(a_part, "row")
-    b = lax.psum(b_part, "col")
+    a, b, s = sums(a_part, b_part, s_part)
     inv = pl.pallas_call(
         inverse_kernel,
         out_shape=jax.ShapeDtypeStruct((nobs, nobs), jnp.float32),

time: 467 us -> 308 us (0.66)
  waiting for transfers between devices: 261 us -> 81.9 us
  Pallas kernels: 111 us -> 165 us
  between operations: 15.2 us -> 0.41 us
  local copies, waits for them, and re-layouts: 24.8 us -> 13.6 us
  starting transfers between devices: 34.6 us -> 25.3 us
    psum x3 -> x0, waiting for transfers between devices: 253 us -> none  [the longest x1 156 us: shards(): s = lax.psum(s_part, ('row', 'col'))]
    ppermute x3, waiting for transfers between devices: 2.32 us -> 73.3 us  [halos(): lax.ppermute(head, axis, [(i + hop, i) for i in range(count - hop)])]
    pallas_call x0 -> x1, Pallas kernels: none -> 70.5 us  [sums(): pl.pallas_call(functools.partial(sums_kernel, sizes), in_specs=[vmem] * 3...]
    pallas_call x2, Pallas kernels: 22.7 us -> 7.5 us  [site_rows(): pl.pallas_call(site_kernel, grid_spec=pltpu.PrefetchScalarGridSpec(num_sc...]
    ppermute x3, starting transfers between devices: 19 us -> 11.5 us  [halos(): lax.ppermute(tail, axis, [(i, i + hop) for i in range(count - hop)])]
    unnamed x48 -> x22, local copies, waits for them, and re-layouts: 8.68 us -> 2.14 us
  transfers between devices with their start and end apart: 13 -> 10, of which waited for: 5 -> 2; matrix products, arithmetic and copies ran while one was open for 5% -> 9% of each run, Pallas kernels for 13% -> 46%
where the time goes in v2:
time: 308 us; the launch traced here: 304 us
  Pallas kernels  165 us (54%)
  waiting for transfers between devices  81.9 us (27%)
  starting transfers between devices  25.3 us (8%)
  matrix products  15.4 us (5%)
  local copies, waits for them, and re-layouts  13.6 us (4%)
    ppermute x3, waiting for transfers between devices, halos(): lax.ppermute(head, axis, [(i + hop, i) for i in range(count - hop)])  73.3 us
    pallas_call x1, Pallas kernels, sums(): pl.pallas_call(functools.partial(sums_kernel, sizes), in_specs=[vmem] * 3...  70.5 us
    pallas_call x1, Pallas kernels, shards(): pl.pallas_call(inverse_kernel, out_shape=jax.ShapeDtypeStruct((nobs, nobs...  32 us
    pallas_call x1, Pallas kernels, shards(): pl.pallas_call(functools.partial(final_kernel, pieces, len(arrays)), grid...  25.3 us
    pallas_call x3, Pallas kernels, row_transport(): pl.pallas_call(functools.partial(row_kernel, rows // LON), grid=(tiles,),...  25 us
    ppermute x3, starting transfers between devices, halos(): lax.ppermute(tail, axis, [(i, i + hop) for i in range(count - hop)])  11.5 us
    ppermute x3, waiting for transfers between devices, halos(): lax.ppermute(tail, axis, [(i, i + hop) for i in range(count - hop)])  8.62 us
    dot_general x1, matrix products, shards(): a_part = dot(g_row, covariance, (((1,), (0,)), ((), ())))  7.58 us
  transfers between devices with their start and end apart: 10, of which 2 were waited for; matrix products, arithmetic and copies ran while one was open for 9% of the time, Pallas kernels for 46%

profile of v2, /device:TPU:0, one launch (start us, length us, event | category | flops | bytes accessed | tf_op | source)
XLA Modules:
  0.0 304.5 jit_solution(5461457754326199236)
XLA Ops:
  0.0 1.8 fusion.6
  2.9 2.4 collective-permute-start
  6.5 1.4 collective-permute-start.1
  7.9 4.2 %fusion.5 = (f32[384,1280]{1,0:T(8,128)}, f32[384,1280]{1,0:T(8,128)}) fusion(f32[1024,2048]{1,0:T(8,128)} %x.5), kind=kLoop, calls=%fused_computation.15 | loop fusion | bytes 7864320 | tf_op jit(solution)/shard_map/slice | solution.py:30
  13.4 5.9 %collective-permute-start.3 = (f32[384,1280]{1,0:T(8,128)}, f32[384,1280]{1,0:T(8,128)S(1)}, u32[]{:S(2)}, u32[]{:S(2)}) collective-permute-start(f32[384,1280]{1,0:T(8,128)} %get-tuple-element.20), channel_id=1, source_target_pairs={{0,4},{4,8},{8,12},{12,16},{16,20},{20,24},{24,28},{1,5},{5,9},{9,... | collective-permute-start | bytes 5898248 | tf_op jit(solution)/shard_map/ppermute | solution.py:31
  19.9 2.8 shard_map.75
  22.7 7.6 %fusion.11.a = f32[256,2048]{1,0:T(8,128)} fusion(f32[256,1024]{1,0:T(8,128)S(1)} %shard_map.75, f32[1024,2048]{1,0:T(8,128)} %x.5), kind=kOutput, calls=%fused_computation.21 | convolution fusion | flops 3221225472 | bytes 11534336 | tf_op jit(solution)/shard_map/dot_general | solution.py:440
  30.4 4.7 %shard_map.76 = f32[256,2048]{1,0:T(8,128)S(1)} custom-call(s32[1]{0:T(128)} %bitcast.6.start_ref, s32[256,1]{1,0:T(8,128)S(1)} %copy.9.site, f32[1,2816]{1,0:T(1,128)S(1)} %get-tuple-element.34.cu.args_6_, f32[1,2816]{1,0:T(1,128)S(1)} %get-tuple-element.33.cv.args_7_, f32[1,2816]{1,0:T(1,128)S(1)} %get-tuple-element.32.su.args_8_, ...), custom_call_target="tpu_custom_call" | custom-call | tf_op jit(solution)/shard_map/pallas_call | solution.py:179
  35.1 1.9 fusion.12.s
  37.0 6.0 %convolution_bitcast_fusion.b = f32[1024,256]{1,0:T(8,128)S(1)} fusion(f32[256,2048]{1,0:T(8,128)S(1)} %shard_map.76, f32[1024,2048]{1,0:T(8,128)} %x.5), kind=kOutput, calls=%fused_computation | convolution fusion | flops 3221225472 | bytes 11534336 | tf_op jit(solution)/shard_map/dot_general | solution.py:441
  43.0 70.5 %shard_map.77 = (f32[256,2048]{1,0:T(8,128)S(1)}, f32[1024,256]{1,0:T(8,128)S(1)}, f32[256,256]{1,0:T(8,128)S(1)}) custom-call(f32[256,2048]{1,0:T(8,128)} %fusion.11.a, f32[1024,256]{1,0:T(8,128)S(1)} %convolution_bitcast_fusion.b, f32[256,256]{1,0:T(8,128)S(1)} %fusion.12.s), custom_call_target="tpu_custom_call" | custom-call | tf_op jit(solution)/shard_map/pallas_call | solution.py:358
  113.6 1.5 collective-permute-start.7
  116.3 8.6 %shard_map.73.args_1_ = f32[1024,768]{1,0:T(8,128)} custom-call(f32[1024,2048]{1,0:T(8,128)} %x.5, f32[384,768]{1,0:T(8,128)S(1)} %collective-permute-done.lo, f32[384,768]{1,0:T(8,128)} %collective-permute-done.1.hi, f32[1792,128]{1,0:T(8,128)S(1)} %broadcast_in_dim.29.cu, f32[1792,128]{1,0:T(8,128)S(1)} %broadcast_in_dim.31.cv, ...), custom_call_target="tpu_custom_call" | custom-call | flops 41287680 | bytes 11010048 | tf_op jit(solution)/shard_map/pallas_call | solution.py:72
  124.9 3.8 %fusion.7 = (f32[1024,384]{1,0:T(8,128)}, f32[1024,384]{1,0:T(8,128)}) fusion(f32[1024,768]{1,0:T(8,128)} %shard_map.73.args_1_), kind=kLoop, calls=%fused_computation.17 | loop fusion | bytes 6291456 | tf_op jit(solution)/shard_map/slice | solution.py:419
  130.0 4.6 %collective-permute-start.2 = (f32[1024,384]{1,0:T(8,128)}, f32[1024,384]{1,0:T(8,128)S(1)}, u32[]{:S(2)}, u32[]{:S(2)}) collective-permute-start(f32[1024,384]{1,0:T(8,128)} %get-tuple-element.26), channel_id=1, source_target_pairs={{0,1},{1,2},{2,3},{4,5},{5,6},{6,7},{8,9},{9,10},{10,11},{12,13},{... | collective-permute-start | bytes 4718600 | tf_op jit(solution)/shard_map/ppermute | solution.py:421
  136.7 73.3 %collective-permute-done.9.hi = f32[256,384]{1,0:T(8,128)S(1)} collective-permute-done((f32[256,384]{1,0:T(8,128)S(1)}, f32[256,384]{1,0:T(8,128)S(1)}, u32[]{:S(2)}, u32[]{:S(2)}) %collective-permute-start.9) | collective-permute-done | bytes 393248 | tf_op jit(solution)/shard_map/ppermute | solution.py:32
  210.0 4.3 %collective-permute-start.8 = (f32[256,384]{1,0:T(8,128)S(1)}, f32[256,384]{1,0:T(8,128)S(1)}, u32[]{:S(2)}, u32[]{:S(2)}) collective-permute-start(f32[256,384]{1,0:T(8,128)S(1)} %get-tuple-element.28), channel_id=1, source_target_pairs={{0,1},{1,2},{2,3},{4,5},{5,6},{6,7},{8,9},{9,10},{10,11},{12,13},{... | collective-permute-start | bytes 1179656 | tf_op jit(solution)/shard_map/ppermute | solution.py:31
  214.3 8.6 %collective-permute-done.8.lo = f32[256,384]{1,0:T(8,128)S(1)} collective-permute-done((f32[256,384]{1,0:T(8,128)S(1)}, f32[256,384]{1,0:T(8,128)S(1)}, u32[]{:S(2)}, u32[]{:S(2)}) %collective-permute-start.8) | collective-permute-done | bytes 393248 | tf_op jit(solution)/shard_map/ppermute | solution.py:31
  224.3 32.0 %shard_map.79.inv = f32[256,256]{1,0:T(8,128)S(1)} custom-call(f32[256,256]{1,0:T(8,128)S(1)} %get-tuple-element.10.s, f32[1,256]{1,0:T(1,128)S(1)} %bitcast.16), custom_call_target="tpu_custom_call" | custom-call | tf_op jit(solution)/shard_map/pallas_call | solution.py:446
  256.3 5.1 %shard_map.80.args_5_ = f32[256,2048]{1,0:T(8,128)S(1)} custom-call(f32[256,2048]{1,0:T(8,128)S(1)} %get-tuple-element.9.a, f32[256,384]{1,0:T(8,128)S(1)} %collective-permute-done.8.lo, f32[256,384]{1,0:T(8,128)S(1)} %collective-permute-done.9.hi, f32[256,256]{1,0:T(8,128)S(1)} %shard_map.79.inv, f32[1,2816]{1,0:T(1,128)S(1)} %get-tuple-element.34.cu.args_6_, ...), custom_call_target="tpu_custom_call" | custom-call | tf_op jit(solution)/shard_map/pallas_call | solution.py:455
  261.4 1.4 copy-done
  262.7 3.1 %shard_map.78.args_4_ = f32[1024,256]{1,0:T(8,128)S(1)} custom-call(f32[1024,256]{1,0:T(8,128)} %copy-done.1, f32[384,256]{1,0:T(8,128)S(1)} %collective-permute-done.6.lo, f32[384,256]{1,0:T(8,128)S(1)} %copy-done.3, f32[1792,128]{1,0:T(8,128)S(1)} %broadcast_in_dim.29.cu, f32[1792,128]{1,0:T(8,128)S(1)} %broadcast_in_dim.31.cv, ...), custom_call_target="tpu_custom_call" | custom-call | flops 13762560 | bytes 3670016 | tf_op jit(solution)/shard_map/pallas_call | solution.py:72
  265.9 13.3 %shard_map.74.args_2_ = f32[1024,1280]{1,0:T(8,128)} custom-call(f32[1024,2048]{1,0:T(8,128)} %x.5, f32[384,1280]{1,0:T(8,128)S(1)} %collective-permute-done.3.lo, f32[384,1280]{1,0:T(8,128)} %collective-permute-done.4.hi, f32[1792,128]{1,0:T(8,128)S(1)} %broadcast_in_dim.29.cu, f32[1792,128]{1,0:T(8,128)S(1)} %broadcast_in_dim.31.cv, ...), custom_call_target="tpu_custom_call" | custom-call | flops 68812800 | bytes 18350080 | tf_op jit(solution)/shard_map/pallas_call | solution.py:72
  279.2 25.3 %shard_map.81 = f32[1024,2048]{1,0:T(8,128)} custom-call(f32[1024,384]{1,0:T(8,128)S(1)} %collective-permute-done.2.args_0_, f32[1024,768]{1,0:T(8,128)} %shard_map.73.args_1_, f32[1024,1280]{1,0:T(8,128)} %shard_map.74.args_2_, f32[1024,384]{1,0:T(8,128)S(1)} %collective-permute-done.5.args_3_, f32[1024,256]{1,0:T(8,128)S(1)} %shard_map.78.args_4_, ...), custom_call_target="tpu_custom_call" | custom-call | tf_op jit(solution)/shard_map/pallas_call | solution.py:466
  (47 shorter events, 10.0 us)
Async XLA Ops:
  2.9 112.2 %collective-permute-start = (f32[384,768]{1,0:T(8,128)}, f32[384,768]{1,0:T(8,128)S(1)}, u32[]{:S(2)}, u32[]{:S(2)}) collective-permute-start(f32[384,768]{1,0:T(8,128)} %pad_maximum_fusion), channel_id=1, source_target_pairs={{0,4},{4,8},{8,12},{12,16},{16,20},{20,24},{24,28},{1,5},{5,9},{9,... | collective-permute-start | bytes 3538952 | tf_op jit(solution)/shard_map/ppermute | solution.py:409
  6.5 12.9 %copy-start.8 = (s32[8192]{0:T(1024)S(1)}, s32[8192]{0:T(1024)}, u32[]{:S(2)}) copy-start(s32[8192]{0:T(1024)} %param.10) | copy-start | bytes 98308
  6.5 12.9 %copy-start.9 = (s32[8192]{0:T(1024)S(1)}, s32[8192]{0:T(1024)}, u32[]{:S(2)}) copy-start(s32[8192]{0:T(1024)} %param.11) | copy-start | bytes 98308
  6.5 13.0 %copy-start.10 = (s32[256]{0:T(256)S(1)}, s32[256]{0:T(256)}, u32[]{:S(2)}) copy-start(s32[256]{0:T(256)} %param.12) | copy-start | bytes 3076
  6.5 13.1 %copy-start.6 = (f32[8192]{0:T(1024)S(1)}, f32[8192]{0:T(1024)}, u32[]{:S(2)}) copy-start(f32[8192]{0:T(1024)} %param.9) | copy-start | bytes 98308
  6.5 13.1 %copy-start.7 = (f32[8192]{0:T(1024)S(1)}, f32[8192]{0:T(1024)}, u32[]{:S(2)}) copy-start(f32[8192]{0:T(1024)} %param.8) | copy-start | bytes 98308
  6.5 108.6 %collective-permute-start.1 = (f32[384,768]{1,0:T(8,128)}, f32[384,768]{1,0:T(8,128)}, u32[]{:S(2)}, u32[]{:S(2)}) collective-permute-start(f32[384,768]{1,0:T(8,128)} %pad_maximum_fusion.1), channel_id=1, source_target_pairs={{4,0},{8,4},{12,8},{16,12},{20,16},{24,20},{28,24},{5,1},{9,5},{13... | collective-permute-start | bytes 3538952 | tf_op jit(solution)/shard_map/ppermute | solution.py:410
  12.2 253.7 %collective-permute-start.4 = (f32[384,1280]{1,0:T(8,128)}, f32[384,1280]{1,0:T(8,128)}, u32[]{:S(2)}, u32[]{:S(2)}) collective-permute-start(f32[384,1280]{1,0:T(8,128)} %get-tuple-element.19), channel_id=1, source_target_pairs={{4,0},{8,4},{12,8},{16,12},{20,16},{24,20},{28,24},{5,1},{9,5},{13... | collective-permute-start | bytes 5898248 | tf_op jit(solution)/shard_map/ppermute | solution.py:32
  13.4 252.4 %collective-permute-start.3 = (f32[384,1280]{1,0:T(8,128)}, f32[384,1280]{1,0:T(8,128)S(1)}, u32[]{:S(2)}, u32[]{:S(2)}) collective-permute-start(f32[384,1280]{1,0:T(8,128)} %get-tuple-element.20), channel_id=1, source_target_pairs={{0,4},{4,8},{8,12},{12,16},{16,20},{20,24},{24,28},{1,5},{5,9},{9,... | collective-permute-start | bytes 5898248 | tf_op jit(solution)/shard_map/ppermute | solution.py:31
  30.3 4.8 %copy-start.5 = (f32[256,2048]{1,0:T(8,128)S(1)}, f32[256,2048]{1,0:T(8,128)}, u32[]{:S(2)}) copy-start(f32[256,2048]{1,0:T(8,128)} %fusion.11.a) | copy-start | bytes 6291460
  113.5 2.5 copy-start.1
  113.6 21.1 %collective-permute-start.7 = (f32[384,256]{1,0:T(8,128)S(1)}, f32[384,256]{1,0:T(8,128)S(1)}, u32[]{:S(2)}, u32[]{:S(2)}) collective-permute-start(f32[384,256]{1,0:T(8,128)S(1)} %get-tuple-element.29), channel_id=1, source_target_pairs={{4,0},{8,4},{12,8},{16,12},{20,16},{24,20},{28,24},{5,1},{9,5},{13... | collective-permute-start | bytes 1179656 | tf_op jit(solution)/shard_map/ppermute | solution.py:32
  124.9 99.4 %copy-start.4 = (f32[256]{0:T(256)S(1)}, f32[256]{0:T(256)}, u32[]{:S(2)}) copy-start(f32[256]{0:T(256)} %param.13) | copy-start | bytes 3076
  128.7 150.5 %collective-permute-start.5 = (f32[1024,384]{1,0:T(8,128)}, f32[1024,384]{1,0:T(8,128)S(1)}, u32[]{:S(2)}, u32[]{:S(2)}) collective-permute-start(f32[1024,384]{1,0:T(8,128)} %get-tuple-element.25), channel_id=1, source_target_pairs={{1,0},{2,1},{3,2},{5,4},{6,5},{7,6},{9,8},{10,9},{11,10},{13,12},{... | collective-permute-start | bytes 4718600 | tf_op jit(solution)/shard_map/ppermute | solution.py:422
  130.0 149.2 %collective-permute-start.2 = (f32[1024,384]{1,0:T(8,128)}, f32[1024,384]{1,0:T(8,128)S(1)}, u32[]{:S(2)}, u32[]{:S(2)}) collective-permute-start(f32[1024,384]{1,0:T(8,128)} %get-tuple-element.26), channel_id=1, source_target_pairs={{0,1},{1,2},{2,3},{4,5},{5,6},{6,7},{8,9},{9,10},{10,11},{12,13},{... | collective-permute-start | bytes 4718600 | tf_op jit(solution)/shard_map/ppermute | solution.py:421
  134.7 0.7 copy-start.2
  135.4 74.6 %collective-permute-start.9 = (f32[256,384]{1,0:T(8,128)S(1)}, f32[256,384]{1,0:T(8,128)S(1)}, u32[]{:S(2)}, u32[]{:S(2)}) collective-permute-start(f32[256,384]{1,0:T(8,128)S(1)} %get-tuple-element.27), channel_id=1, source_target_pairs={{1,0},{2,1},{3,2},{5,4},{6,5},{7,6},{9,8},{10,9},{11,10},{13,12},{... | collective-permute-start | bytes 1179656 | tf_op jit(solution)/shard_map/ppermute | solution.py:32
  210.0 12.9 %collective-permute-start.8 = (f32[256,384]{1,0:T(8,128)S(1)}, f32[256,384]{1,0:T(8,128)S(1)}, u32[]{:S(2)}, u32[]{:S(2)}) collective-permute-start(f32[256,384]{1,0:T(8,128)S(1)} %get-tuple-element.28), channel_id=1, source_target_pairs={{0,1},{1,2},{2,3},{4,5},{5,6},{6,7},{8,9},{9,10},{10,11},{12,13},{... | collective-permute-start | bytes 1179656 | tf_op jit(solution)/shard_map/ppermute | solution.py:31
  223.0 39.8 %collective-permute-start.6 = (f32[384,256]{1,0:T(8,128)S(1)}, f32[384,256]{1,0:T(8,128)S(1)}, u32[]{:S(2)}, u32[]{:S(2)}) collective-permute-start(f32[384,256]{1,0:T(8,128)S(1)} %get-tuple-element.30), channel_id=1, source_target_pairs={{0,4},{4,8},{8,12},{12,16},{16,20},{20,24},{24,28},{1,5},{5,9},{9,... | collective-permute-start | bytes 1179656 | tf_op jit(solution)/shard_map/ppermute | solution.py:31
  256.3 6.5 %copy-start.3 = (f32[384,256]{1,0:T(8,128)S(1)}, f32[384,256]{1,0:T(8,128)}, u32[]{:S(2)}) copy-start(f32[384,256]{1,0:T(8,128)} %copy-done.2) | copy-start | bytes 1179652
  261.4 1.4 copy-start

commit v3 on v2

--- a/solution.py
+++ b/solution.py
@@ -19,25 +19,31 @@
     return pltpu.CompilerParams(vmem_limit_bytes=VMEM_LIMIT)
 
 
-def halos(x, axis, dim):
+def halos(xs, axis, dim):
     count = lax.axis_size(axis)
-    size = x.shape[dim]
+    size = xs[0].shape[dim]
     before, after = [], []
     left, hop = MARGIN, 1
+
+    def part(lo, hi):
+        return jnp.concatenate([lax.slice_in_dim(x, lo, hi, axis=dim) for x in xs], axis=1 - dim)
+
     while left > 0:
         take = min(left, size)
-        tail = lax.slice_in_dim(x, size - take, size, axis=dim)
-        head = lax.slice_in_dim(x, 0, take, axis=dim)
+        tail, head = part(size - take, size), part(0, take)
         before.insert(0, lax.ppermute(tail, axis, [(i, i + hop) for i in range(count - hop)]))
         after.append(lax.ppermute(head, axis, [(i + hop, i) for i in range(count - hop)]))
         left, hop = left - take, hop + 1
-    if len(before) == 1:
-        return before[0], after[0]
     return jnp.concatenate(before, axis=dim), jnp.concatenate(after, axis=dim)
 
 
 def advance(q, minus, plus, cu, cv, su, sv, dim):
-    lon = jnp.where(su > 0, pltpu.roll(q, 1, dim), pltpu.roll(q, LON - 1, dim))
+    if dim == 1:
+        lane = lax.broadcasted_iota(jnp.int32, q.shape, 1)
+        step = jnp.where(su > 0, LON - 1, 1)
+        lon = jnp.take_along_axis(q, (lane + step) & (LON - 1), axis=1, mode="promise_in_bounds")
+    else:
+        lon = jnp.where(su > 0, pltpu.roll(q, 1, dim), pltpu.roll(q, LON - 1, dim))
     lat = jnp.where(sv > 0, minus, plus)
     return q - cu * (q - lon) - cv * (q - lat)
 
@@ -86,7 +92,7 @@
         scratch_shapes=[pltpu.VMEM((2, wide, LON), jnp.float32)],
         compiler_params=params(),
         cost_estimate=pl.CostEstimate(
-            flops=30 * wide * tiles * LON, bytes_accessed=8 * wide * tiles * LON, transcendentals=0
+            flops=30 * wide * tiles * LON, bytes_accessed=24 * wide * tiles * LON, transcendentals=0
         ),
     )(x, lo, hi, *coeffs)
 
@@ -115,9 +121,10 @@
 
 
 def final_kernel(pieces, n, *args):
-    refs, (pht, w, cu, cv, su, sv, out, buf) = args[:n], args[n:]
+    refs, (pht, w_hi, w_lo, cu, cv, su, sv, out, buf) = args[:n], args[n:]
     raw, total = band_reader([(refs[i], f, c) for i, f, c in pieces])
-    gain = pht[...]
+    hi, lo = halves(pht[...])
+    dot = functools.partial(jnp.dot, preferred_element_type=jnp.float32)
 
     def finish(k, new):
         c = slice(k * LON, (k + 1) * LON)
@@ -125,21 +132,20 @@
 
     for c in range(0, out.shape[1], 512):
         d = slice(c, min(c + 512, out.shape[1]))
-        out[:, d] = jnp.dot(gain, w[:, d], precision=HIGHEST, preferred_element_type=jnp.float32)
+        out[:, d] = dot(hi, w_hi[:, d]) + (dot(lo, w_hi[:, d]) + dot(hi, w_lo[:, d]))
     col_steps(raw, total, cu, cv, su, sv, buf, finish)
 
 
-def weights_kernel(a, lo, hi, inv, cu, cv, su, sv, w, hp, buf):
-    bands = a.shape[1] // LON
-    raw, total = band_reader([(lo, 0, STEPS), (a, 0, bands), (hi, 0, STEPS)])
+def weights_kernel(a, inv, cu, cv, su, sv, w_hi, w_lo, hp, buf):
+    raw, total = band_reader([(a, 0, a.shape[1] // LON)])
 
     def finish(k, new):
         hp[:, k * LON : (k + 1) * LON] = new
 
     col_steps(raw, total, cu, cv, su, sv, buf, finish)
-    for c in range(0, w.shape[1], 512):
-        d = slice(c, min(c + 512, w.shape[1]))
-        w[:, d] = jnp.dot(inv[...], hp[:, d], precision=HIGHEST, preferred_element_type=jnp.float32)
+    for c in range(0, hp.shape[1], 512):
+        d = slice(c, min(c + 512, hp.shape[1]))
+        w_hi[:, d], w_lo[:, d] = halves(mm(inv[...], hp[:, d]))
 
 
 def site_kernel(start_ref, site, cu, cv, su, sv, out):
@@ -189,7 +195,7 @@
     )(start.reshape(1).astype(jnp.int32), site.reshape(nobs, 1), *coeffs)
 
 
-def sweep_inverse(a):
+def sweep_inverse(a, tick):
     n = a.shape[0]
     sub = lax.broadcasted_iota(jnp.int32, (n, n), 0)
     lane = lax.broadcasted_iota(jnp.int32, (n, n), 1)
@@ -204,22 +210,30 @@
         a = jnp.concatenate([a[8:], a[:8]], axis=0)
         return pltpu.roll(a, n - 8, 1)
 
-    return -lax.fori_loop(0, n // 8, body, a)
+    for _ in range(2):
+        a = lax.fori_loop(0, n // 16, body, a)
+        tick()
+    return -a
+
+
+def halves(x):
+    hi = x.astype(jnp.bfloat16)
+    return hi, (x - hi.astype(jnp.float32)).astype(jnp.bfloat16)
 
 
 def mm(x, y):
     return jnp.dot(x, y, precision=HIGHEST, preferred_element_type=jnp.float32)
 
 
-def inverse(a):
+def inverse(a, tick):
     n = a.shape[0]
     if n <= LON:
-        return sweep_inverse(a)
+        return sweep_inverse(a, tick)
     h = n // 2
     s12, s22 = a[:h, h:], a[h:, h:]
-    i1 = inverse(a[:h, :h])
+    i1 = inverse(a[:h, :h], tick)
     x = mm(i1, s12)
-    i2 = inverse(s22 - mm(s12.T, x))
+    i2 = inverse(s22 - mm(s12.T, x), tick)
     y = mm(x, i2)
     return jnp.concatenate(
         [
@@ -228,14 +242,6 @@
         ],
         axis=0,
     )
-
-
-def inverse_kernel(s, r, out):
-    n = s.shape[0]
-    sub = lax.broadcasted_iota(jnp.int32, (n, n), 0)
-    lane = lax.broadcasted_iota(jnp.int32, (n, n), 1)
-    a = s[...] + jnp.where(sub == lane, jnp.broadcast_to(r[...], (n, n)), 0.0)
-    out[...] = inverse(0.5 * (a + a.T))
 
 
 def partner_of(axis, d):
@@ -296,20 +302,91 @@
     yield from all_gather(out, off, size, axis, count, sems, base + len(powers(count)))
 
 
-def butterfly(acc, rx, sizes, sems, base):
-    t = 0
-    for axis, count in sizes:
-        for d in powers(count):
-            _, peer = partner_of(axis, d)
-            copy = exchange(acc.at[t], rx.at[t], axis, peer, sems, base + t)
-            copy.start()
-            yield
-            copy.wait()
-            acc[t + 1] = acc[t] + rx[t]
-            t += 1
-
-
-def sums_kernel(sizes, a, b, s, a_out, b_out, s_out, a_acc, a_rx, a_all, b_acc, b_rx, b_all, s_acc, s_rx, sems):
+def small_reduce(acc, rx, part, part_rx, out, first, rest, sems, base):
+    off, size, at, i = 0, acc.shape[0], 0, base
+    for axis, d in first:
+        bit, peer = partner_of(axis, d)
+        half = size // 2
+        keep = pl.multiple_of(off + bit * half, 8)
+        give = pl.multiple_of(off + (1 - bit) * half, 8)
+        copy = exchange(
+            acc.at[pl.ds(give, half), :], rx.at[at : at + half, :], axis, peer, sems, i
+        )
+        copy.start()
+        yield
+        copy.wait()
+        acc[pl.ds(keep, half), :] += rx[at : at + half, :]
+        off, size, at, i = keep, half, at + half, i + 1
+    own = pl.ds(pl.multiple_of(off, 8), size)
+    part[0] = acc[own, :]
+    for t, (axis, d) in enumerate(rest):
+        _, peer = partner_of(axis, d)
+        copy = exchange(part.at[t], part_rx.at[t], axis, peer, sems, i)
+        copy.start()
+        yield
+        copy.wait()
+        part[t + 1] = part[t] + part_rx[t]
+        i += 1
+    out[own, :] = part[len(rest)]
+    for axis, d in reversed(first):
+        bit, peer = partner_of(axis, d)
+        ref = out.at[pl.ds(pl.multiple_of(off, 8), size), :]
+        copy = exchange(ref, ref, axis, peer, sems, i)
+        copy.start()
+        yield
+        copy.wait()
+        off, size, i = off - bit * size, size * 2, i + 1
+
+
+class Edges:
+    def __init__(self, first, last, from_prev, from_next, axis, count, sems, i):
+        me = lax.axis_index(axis)
+        self.has_next, self.has_prev = me < count - 1, me > 0
+        self.into = from_prev, from_next
+        self.up = exchange(last, from_prev, axis, jnp.minimum(me + 1, count - 1), sems, i)
+        self.down = exchange(first, from_next, axis, jnp.maximum(me - 1, 0), sems, i + 1)
+
+    def start(self):
+        @pl.when(self.has_next)
+        def _():
+            self.up.start()
+
+        @pl.when(self.has_prev)
+        def _():
+            self.down.start()
+
+    def finish(self):
+        @pl.when(self.has_next)
+        def _():
+            self.up.wait_send()
+            self.down.wait_recv()
+
+        @pl.when(self.has_prev)
+        def _():
+            self.down.wait_send()
+            self.up.wait_recv()
+
+        @pl.when(jnp.logical_not(self.has_prev))
+        def _():
+            self.into[0][...] = jnp.zeros(self.into[0].shape, jnp.float32)
+
+        @pl.when(jnp.logical_not(self.has_next))
+        def _():
+            self.into[1][...] = jnp.zeros(self.into[1].shape, jnp.float32)
+
+
+def advance_all(live):
+    for run in list(live):
+        try:
+            next(run)
+        except StopIteration:
+            live.remove(run)
+
+
+def sums_kernel(
+    sizes, a, b, s, r, edges, a_out, b_out, inv_out, beside,
+    a_acc, a_rx, a_all, b_acc, b_rx, b_all, s_acc, s_rx, s_part, s_part_rx, s_all, a_side, sems,
+):
     barrier = pltpu.get_barrier_semaphore()
     greeted = 0
     for axis, count in sizes:
@@ -319,47 +396,92 @@
                 barrier, inc=1, device_id={axis: peer}, device_id_type=pl.DeviceIdType.MESH
             )
             greeted += 1
+    (row, rows), (col, cols) = sizes
+    place = lax.axis_index(col)
+    for near in ((place + 1) % cols, (place + cols - 1) % cols):
+        pl.semaphore_signal(
+            barrier, inc=1, device_id={col: near}, device_id_type=pl.DeviceIdType.MESH
+        )
+        greeted += 1
     pl.semaphore_wait(barrier, greeted)
-    (row, rows), (col, cols) = sizes
     nobs = s.shape[0]
     tiles = a.shape[1] // LON
-    s_acc[0] = s[...]
+    s_acc[...] = s[...]
+    first, rest = small_order(sizes)
+    n_row, n_col = len(powers(rows)), len(powers(cols))
+    used = 2 * len(first) + len(rest)
+    last = used + 2 * (n_row + n_col)
+    wide = Edges(
+        edges.at[:, :MARGIN], edges.at[:, edges.shape[1] - MARGIN :], beside.at[:, :MARGIN], beside.at[:, MARGIN:],
+        col, cols, sems, last,
+    )
+    small = [small_reduce(s_acc, s_rx, s_part, s_part_rx, s_all, first, rest, sems, 0)]
+    advance_all(small)
+    wide.start()
     for k in range(tiles):
         a_acc[k * nobs : (k + 1) * nobs, :] = a[:, k * LON : (k + 1) * LON]
     b_acc[...] = b[...]
-    n_row, n_col = len(powers(rows)), len(powers(cols))
-    live = [
-        butterfly(s_acc, s_rx, sizes, sems, 0),
-        all_reduce(a_acc, a_rx, a_all, row, rows, sems, n_row + n_col),
-        all_reduce(b_acc, b_rx, b_all, col, cols, sems, 3 * n_row + n_col),
+    large = [
+        all_reduce(a_acc, a_rx, a_all, row, rows, sems, used),
+        all_reduce(b_acc, b_rx, b_all, col, cols, sems, used + 2 * n_row),
     ]
-    while live:
-        still = []
-        for run in live:
-            try:
-                next(run)
-                still.append(run)
-            except StopIteration:
-                pass
-        live = still
-    s_out[...] = s_acc[n_row + n_col]
+    advance_all(large)
+    step = 0
+    while small:
+        advance_all(small)
+        step += 1
+        if step % 3 == 0:
+            advance_all(large)
+    sub = lax.broadcasted_iota(jnp.int32, (nobs, nobs), 0)
+    lane = lax.broadcasted_iota(jnp.int32, (nobs, nobs), 1)
+    m = s_all[...] + jnp.where(sub == lane, jnp.broadcast_to(r[...], (nobs, nobs)), 0.0)
+    inv_out[...] = inverse(0.5 * (m + m.T), lambda: advance_all(large))
+    while large:
+        advance_all(large)
+    reach = STEPS * nobs
+    narrow = Edges(
+        a_all.at[:reach, :], a_all.at[(tiles - STEPS) * nobs :, :], a_side.at[0], a_side.at[1],
+        col, cols, sems, last + 2,
+    )
+    narrow.start()
     b_out[...] = b_all[...]
     for k in range(tiles):
-        a_out[:, k * LON : (k + 1) * LON] = a_all[k * nobs : (k + 1) * nobs, :]
-
-
-def sums(a, b, s):
+        c = MARGIN + k * LON
+        a_out[:, c : c + LON] = a_all[k * nobs : (k + 1) * nobs, :]
+    narrow.finish()
+    for k in range(STEPS):
+        c = MARGIN + (tiles + k) * LON
+        a_out[:, k * LON : (k + 1) * LON] = a_side[0, k * nobs : (k + 1) * nobs, :]
+        a_out[:, c : c + LON] = a_side[1, k * nobs : (k + 1) * nobs, :]
+    wide.finish()
+
+
+def small_order(sizes):
+    (row, rows), (col, cols) = sizes
+    row_powers = powers(rows)
+    first = [(row, d) for d in row_powers[:1]] + [(col, d) for d in powers(cols)]
+    return first, [(row, d) for d in row_powers[1:]]
+
+
+def sums(a, b, s, r, edges):
     sizes = [(axis, lax.axis_size(axis)) for axis in ("row", "col")]
-    stages = [len(powers(n)) for _, n in sizes]
+    first, rest = small_order(sizes)
+    copies = 2 * len(first) + len(rest) + 2 * sum(len(powers(n)) for _, n in sizes) + 4
     nobs = s.shape[0]
+    part = nobs >> len(first)
     tall = a.shape[0] * a.shape[1] // LON
     vmem = pl.BlockSpec(memory_space=pltpu.VMEM)
     f32 = jnp.float32
     return pl.pallas_call(
         functools.partial(sums_kernel, sizes),
-        in_specs=[vmem] * 3,
-        out_specs=[vmem] * 3,
-        out_shape=[jax.ShapeDtypeStruct(x.shape, f32) for x in (a, b, s)],
+        in_specs=[vmem] * 5,
+        out_specs=[vmem] * 4,
+        out_shape=[
+            jax.ShapeDtypeStruct(shape, f32)
+            for shape in (
+                (nobs, a.shape[1] + 2 * MARGIN), b.shape, s.shape, (b.shape[0], 2 * MARGIN)
+            )
+        ],
         scratch_shapes=[
             pltpu.VMEM((tall, LON), f32),
             pltpu.VMEM((tall, LON), f32),
@@ -367,14 +489,21 @@
             pltpu.VMEM(b.shape, f32),
             pltpu.VMEM(b.shape, f32),
             pltpu.VMEM(b.shape, f32),
-            pltpu.VMEM((sum(stages) + 1, nobs, nobs), f32),
-            pltpu.VMEM((sum(stages), nobs, nobs), f32),
-            pltpu.SemaphoreType.DMA((2, 3 * sum(stages))),
+            pltpu.VMEM(s.shape, f32),
+            pltpu.VMEM(s.shape, f32),
+            pltpu.VMEM((len(rest) + 1, part, nobs), f32),
+            pltpu.VMEM((max(len(rest), 1), part, nobs), f32),
+            pltpu.VMEM(s.shape, f32),
+            pltpu.VMEM((2, STEPS * nobs, LON), f32),
+            pltpu.SemaphoreType.DMA((2, copies)),
         ],
         compiler_params=pltpu.CompilerParams(
             collective_id=0, has_side_effects=True, vmem_limit_bytes=VMEM_LIMIT
         ),
-    )(a, b, s)
+        cost_estimate=pl.CostEstimate(
+            flops=2 * nobs**3, bytes_accessed=80 * a.size * 4, transcendentals=nobs
+        ),
+    )(a, b, s, r, edges)
 
 
 def shards(
@@ -397,40 +526,25 @@
     ]
 
     tiles = cols // LON
-    split = tiles > 2 * STEPS
-    if split:
-        edge_cols = jnp.concatenate([covariance[:, :MARGIN], covariance[:, cols - MARGIN :]], axis=1) if rows < MARGIN else None
-        if edge_cols is None:
-            head = jnp.concatenate([covariance[:MARGIN, :MARGIN], covariance[:MARGIN, cols - MARGIN :]], axis=1)
-            tail = jnp.concatenate(
-                [covariance[rows - MARGIN :, :MARGIN], covariance[rows - MARGIN :, cols - MARGIN :]], axis=1
-            )
-            count = lax.axis_size("row")
-            edge_lo = lax.ppermute(tail, "row", [(i, i + 1) for i in range(count - 1)])
-            edge_hi = lax.ppermute(head, "row", [(i + 1, i) for i in range(count - 1)])
-        else:
-            edge_lo, edge_hi = halos(edge_cols, "row", 0)
-        mid_lo, mid_hi = halos(covariance[:, MARGIN : cols - MARGIN], "row", 0)
+    if tiles > 2 * STEPS:
+        ends = slice(0, MARGIN), slice(cols - MARGIN, cols)
+        edge_lo, edge_hi = halos([covariance[:, c] for c in ends], "row", 0)
+        mid_lo, mid_hi = halos([covariance[:, MARGIN : cols - MARGIN]], "row", 0)
         skip = tiles - 2 * STEPS
         edges = row_transport(
             covariance, edge_lo, edge_hi, row_coeffs, 2 * STEPS,
             lambda j: jnp.where(j < STEPS, j, j + skip),
         )
-        first, last = edges[:, :MARGIN], edges[:, MARGIN:]
-        count = lax.axis_size("col")
-        left = lax.ppermute(last, "col", [(i, i + 1) for i in range(count - 1)])
-        right = lax.ppermute(first, "col", [(i + 1, i) for i in range(count - 1)])
         middle = row_transport(
             covariance, mid_lo, mid_hi, row_coeffs, skip, lambda j: j + STEPS
         )
-        arrays = [left, edges, middle, right]
-        pieces = [(0, 0, STEPS), (1, 0, STEPS), (2, 0, skip), (1, STEPS, STEPS), (3, 0, STEPS)]
+        extra = [middle]
+        inner = [(1, 0, STEPS), (2, 0, skip), (1, STEPS, STEPS)]
     else:
-        lo, hi = halos(covariance, "row", 0)
-        whole = row_transport(covariance, lo, hi, row_coeffs, tiles, lambda j: j)
-        left, right = halos(whole, "col", 1)
-        arrays = [left, whole, right]
-        pieces = [(0, 0, STEPS), (1, 0, tiles), (2, 0, STEPS)]
+        edges = row_transport(
+            covariance, *halos([covariance], "row", 0), row_coeffs, tiles, lambda j: j
+        )
+        extra, inner = [], [(1, 0, tiles)]
 
     g_row = site_rows(measurement_site_position, row_start, row_lines)
     g_col = site_rows(measurement_site_position, col_start, col_lines)
@@ -442,25 +556,21 @@
     s_part = lax.dot_general(
         a_part, g_col, (((1,), (1,)), ((), ())), precision=HIGHEST, preferred_element_type=jnp.float32
     )
-    a, b, s = sums(a_part, b_part, s_part)
-    inv = pl.pallas_call(
-        inverse_kernel,
-        out_shape=jax.ShapeDtypeStruct((nobs, nobs), jnp.float32),
-        compiler_params=params(),
-    )(s, obs_var.reshape(1, nobs))
-    b_lo, b_hi = halos(b, "row", 0)
+    a, b, inv, beside = sums(a_part, b_part, s_part, obs_var.reshape(1, nobs), edges)
+    arrays = [beside, edges] + extra
+    pieces = [(0, 0, STEPS)] + inner + [(0, STEPS, STEPS)]
+    b_lo, b_hi = halos([b], "row", 0)
     pht = row_transport(b, b_lo, b_hi, row_coeffs, nobs // LON, lambda j: j)
-    a_lo, a_hi = halos(a, "col", 1)
     wide = cols + 2 * MARGIN
-    w = pl.pallas_call(
+    w_hi, w_lo = pl.pallas_call(
         weights_kernel,
-        out_shape=jax.ShapeDtypeStruct((nobs, cols), jnp.float32),
+        out_shape=[jax.ShapeDtypeStruct((nobs, cols), jnp.bfloat16)] * 2,
         scratch_shapes=[
             pltpu.VMEM((nobs, cols), jnp.float32),
             pltpu.VMEM((2, nobs, wide), jnp.float32),
         ],
         compiler_params=params(),
-    )(a, a_lo, a_hi, inv, *col_lines)
+    )(a, inv, *col_lines)
 
     tile = LON
     return pl.pallas_call(
@@ -470,13 +580,14 @@
         + [
             pl.BlockSpec((tile, nobs), lambda i: (i, 0)),
             pl.BlockSpec((nobs, cols), lambda i: (0, 0)),
+            pl.BlockSpec((nobs, cols), lambda i: (0, 0)),
         ]
         + [pl.BlockSpec((1, wide), lambda i: (0, 0))] * 4,
         out_specs=pl.BlockSpec((tile, cols), lambda i: (i, 0)),
         out_shape=jax.ShapeDtypeStruct((rows, cols), jnp.float32),
         scratch_shapes=[pltpu.VMEM((2, tile, wide), jnp.float32)],
         compiler_params=params(),
-    )(*arrays, pht, w, *col_lines)
+    )(*arrays, pht, w_hi, w_lo, *col_lines)
 
 
 def solution(mesh):

time: 308 us -> 270 us (0.88)
  waiting for transfers between devices: 81.9 us -> 0.02 us
  Pallas kernels: 165 us -> 225 us
  starting transfers between devices: 25.3 us -> 15.4 us
  local copies, waits for them, and re-layouts: 13.6 us -> 9.58 us
    ppermute x3, waiting for transfers between devices: 73.3 us -> 0.01 us  [halos(): lax.ppermute(head, axis, [(i + hop, i) for i in range(count - hop)])]
    pallas_call x3 -> x2, Pallas kernels: 108 us -> 178 us  [the longest x1 174 us: sums(): pl.pallas_call(functools.partial(sums_kernel, sizes), in_specs=[vmem] * 5...]
    pallas_call x1, Pallas kernels: 25.3 us -> 14.8 us  [shards(): pl.pallas_call(functools.partial(final_kernel, pieces, len(arrays)), grid...]
    ppermute x4 -> x0, starting transfers between devices: 9.77 us -> none  [the longest x1 4.65 us: shards(): left = lax.ppermute(last, 'col', [(i, i + 1) for i in range(count - 1)])]
    ppermute x3, waiting for transfers between devices: 8.62 us -> 0.01 us  [halos(): lax.ppermute(tail, axis, [(i, i + hop) for i in range(count - hop)])]
    slice x6 -> x4, local copies, waits for them, and re-layouts: 10 us -> 6.28 us  [the longest x3 6.15 us: part(): lax.slice_in_dim(x, lo, hi, axis=dim)]
  transfers between devices with their start and end apart: 10 -> 6, of which waited for: 2 -> 0; matrix products, arithmetic and copies ran while one was open for 9% -> 8% of each run, Pallas kernels for 46% -> 74%
where the time goes in v3:
time: 270 us; the launch traced here: 267 us
  Pallas kernels  225 us (83%)
  starting transfers between devices  15.4 us (6%)
  matrix products  14.1 us (5%)
  local copies, waits for them, and re-layouts  9.58 us (4%)
    pallas_call x1, Pallas kernels, sums(): pl.pallas_call(functools.partial(sums_kernel, sizes), in_specs=[vmem] * 5...  174 us
    pallas_call x3, Pallas kernels, row_transport(): pl.pallas_call(functools.partial(row_kernel, rows // LON), grid=(tiles,),...  25 us
    pallas_call x1, Pallas kernels, shards(): pl.pallas_call(functools.partial(final_kernel, pieces, len(arrays)), grid...  14.8 us
    ppermute x3, starting transfers between devices, halos(): lax.ppermute(tail, axis, [(i, i + hop) for i in range(count - hop)])  11.4 us
    pallas_call x2, Pallas kernels, site_rows(): pl.pallas_call(site_kernel, grid_spec=pltpu.PrefetchScalarGridSpec(num_sc...  7.48 us
    dot_general x1, matrix products, shards(): a_part = dot(g_row, covariance, (((1,), (0,)), ((), ())))  6.29 us
    slice x3, local copies, waits for them, and re-layouts, part(): lax.slice_in_dim(x, lo, hi, axis=dim)  6.15 us
    dot_general x1, matrix products, shards(): b_part = dot(covariance, g_col, (((1,), (1,)), ((), ())))  5.91 us
  transfers between devices with their start and end apart: 6, of which 0 were waited for; matrix products, arithmetic and copies ran while one was open for 8% of the time, Pallas kernels for 74%

profile of v3, /device:TPU:0, one launch (start us, length us, event | category | flops | bytes accessed | tf_op | source)
XLA Modules:
  0.0 267.2 jit_solution(10427665058129362065)
XLA Ops:
  0.0 1.8 fusion.6
  1.8 1.1 pad_maximum_fusion
  2.9 2.4 collective-permute-start
  5.3 1.1 pad_maximum_fusion.1
  6.5 1.4 collective-permute-start.1
  7.9 4.3 %fusion.5 = (f32[384,1280]{1,0:T(8,128)}, f32[384,1280]{1,0:T(8,128)}) fusion(f32[1024,2048]{1,0:T(8,128)} %x.5), kind=kLoop, calls=%fused_computation.15 | loop fusion | bytes 7864320 | tf_op jit(solution)/shard_map/slice | solution.py:29
  12.2 1.3 collective-permute-start.3
  13.5 5.9 %collective-permute-start.2 = (f32[384,1280]{1,0:T(8,128)}, f32[384,1280]{1,0:T(8,128)S(1)}, u32[]{:S(2)}, u32[]{:S(2)}) collective-permute-start(f32[384,1280]{1,0:T(8,128)} %get-tuple-element.26), channel_id=1, source_target_pairs={{0,4},{4,8},{8,12},{12,16},{16,20},{20,24},{24,28},{1,5},{5,9},{9,... | collective-permute-start | bytes 5898248 | tf_op jit(solution)/shard_map/ppermute | solution.py:34
  20.1 2.8 %shard_map.73 = f32[256,1024]{1,0:T(8,128)S(1)} custom-call(s32[1]{0:T(128)} %bitcast.start_ref, s32[256,1]{1,0:T(8,128)S(1)} %copy.9.site, f32[1,1792]{1,0:T(1,128)S(1)} %get-tuple-element.42.cu, f32[1,1792]{1,0:T(1,128)S(1)} %get-tuple-element.40.cv, f32[1,1792]{1,0:T(1,128)S(1)} %get-tuple-element.38.su, f32[1,1792]{1,0:T(1,128)S(1)} %get-tuple-element.18.sv), custom_call_target="tpu_custom_call" | custom-call | tf_op jit(solution)/shard_map/pallas_call | solution.py:185
  22.9 4.7 %shard_map.74 = f32[256,2048]{1,0:T(8,128)S(1)} custom-call(s32[1]{0:T(128)} %bitcast.6.start_ref, s32[256,1]{1,0:T(8,128)S(1)} %copy.9.site, f32[1,2816]{1,0:T(1,128)S(1)} %get-tuple-element.36.cu.args_6_, f32[1,2816]{1,0:T(1,128)S(1)} %get-tuple-element.35.cv.args_7_, f32[1,2816]{1,0:T(1,128)S(1)} %get-tuple-element.34.su.args_8_, ...), custom_call_target="tpu_custom_call" | custom-call | tf_op jit(solution)/shard_map/pallas_call | solution.py:185
  27.6 6.3 %fusion.9.a = f32[256,2048]{1,0:T(8,128)S(1)} fusion(f32[256,1024]{1,0:T(8,128)S(1)} %shard_map.73, f32[1024,2048]{1,0:T(8,128)} %x.5), kind=kOutput, calls=%fused_computation.19 | convolution fusion | flops 3221225472 | bytes 11534336 | tf_op jit(solution)/shard_map/dot_general | solution.py:554
  33.9 1.9 fusion.10.s
  35.8 5.9 %convolution_bitcast_fusion.b = f32[1024,256]{1,0:T(8,128)S(1)} fusion(f32[256,2048]{1,0:T(8,128)S(1)} %shard_map.74, f32[1024,2048]{1,0:T(8,128)} %x.5), kind=kOutput, calls=%fused_computation | convolution fusion | flops 3221225472 | bytes 11534336 | tf_op jit(solution)/shard_map/dot_general | solution.py:555
  42.0 0.3 broadcast_in_dim.33.su
  42.3 0.3 broadcast_in_dim.31.cv
  42.9 8.6 %shard_map.75.edges.args_1_ = f32[1024,768]{1,0:T(8,128)} custom-call(f32[1024,2048]{1,0:T(8,128)} %x.5, f32[384,768]{1,0:T(8,128)S(1)} %collective-permute-done.lo, f32[384,768]{1,0:T(8,128)} %collective-permute-done.1.hi, f32[1792,128]{1,0:T(8,128)S(1)} %broadcast_in_dim.29.cu, f32[1792,128]{1,0:T(8,128)S(1)} %broadcast_in_dim.31.cv, ...), custom_call_target="tpu_custom_call" | custom-call | flops 41287680 | bytes 33030144 | tf_op jit(solution)/shard_map/pallas_call | solution.py:78
  51.5 173.9 %shard_map.76 = (f32[256,2816]{1,0:T(8,128)}, f32[1024,256]{1,0:T(8,128)S(1)}, f32[256,256]{1,0:T(8,128)S(1)}, f32[1024,768]{1,0:T(8,128)}) custom-call(f32[256,2048]{1,0:T(8,128)S(1)} %fusion.9.a, f32[1024,256]{1,0:T(8,128)S(1)} %convolution_bitcast_fusion.b, f32[256,256]{1,0:T(8,128)S(1)} %fusion.10.s, f32[1,256]{1,0:T(1,128)S(1)} %bitcast.16, ...), custom_call_target="tpu_custom_call" | custom-call | flops 33554432 | bytes 167772160 | tf_op jit(solution)/shard_map/pallas_call | solution.py:475
  225.6 1.3 collective-permute-start.5
  226.8 3.1 %collective-permute-start.4 = (f32[384,256]{1,0:T(8,128)S(1)}, f32[384,256]{1,0:T(8,128)S(1)}, u32[]{:S(2)}, u32[]{:S(2)}) collective-permute-start(f32[384,256]{1,0:T(8,128)S(1)} %get-tuple-element.32), channel_id=1, source_target_pairs={{0,4},{4,8},{8,12},{12,16},{16,20},{20,24},{24,28},{1,5},{5,9},{9,... | collective-permute-start | bytes 1179656 | tf_op jit(solution)/shard_map/ppermute | solution.py:34
  229.9 1.8 copy-done.1
  231.7 4.3 %shard_map.79 = (bf16[256,2048]{1,0:T(8,128)(2,1)S(1)}, bf16[256,2048]{1,0:T(8,128)(2,1)S(1)}) custom-call(f32[256,2816]{1,0:T(8,128)S(1)} %copy-done.1, f32[256,256]{1,0:T(8,128)S(1)} %get-tuple-element.14.inv, f32[1,2816]{1,0:T(1,128)S(1)} %get-tuple-element.36.cu.args_6_, f32[1,2816]{1,0:T(1,128)S(1)} %get-tuple-element.35.cv.args_7_, ...), custom_call_target="tpu_custom_call" | custom-call | tf_op jit(solution)/shard_map/pallas_call | solution.py:565
  236.0 3.1 %shard_map.78.args_3_ = f32[1024,256]{1,0:T(8,128)S(1)} custom-call(f32[1024,256]{1,0:T(8,128)} %copy-done, f32[384,256]{1,0:T(8,128)S(1)} %collective-permute-done.4.lo, f32[384,256]{1,0:T(8,128)S(1)} %collective-permute-done.5.hi, f32[1792,128]{1,0:T(8,128)S(1)} %broadcast_in_dim.29.cu, f32[1792,128]{1,0:T(8,128)S(1)} %broadcast_in_dim.31.cv, ...), custom_call_target="tpu_custom_call" | custom-call | flops 13762560 | bytes 11010048 | tf_op jit(solution)/shard_map/pallas_call | solution.py:78
  239.2 13.3 %shard_map.77.args_2_ = f32[1024,1280]{1,0:T(8,128)} custom-call(f32[1024,2048]{1,0:T(8,128)} %x.5, f32[384,1280]{1,0:T(8,128)S(1)} %collective-permute-done.2.lo, f32[384,1280]{1,0:T(8,128)} %collective-permute-done.3.hi, f32[1792,128]{1,0:T(8,128)S(1)} %broadcast_in_dim.29.cu, f32[1792,128]{1,0:T(8,128)S(1)} %broadcast_in_dim.31.cv, ...), custom_call_target="tpu_custom_call" | custom-call | flops 68812800 | bytes 55050240 | tf_op jit(solution)/shard_map/pallas_call | solution.py:78
  252.4 14.8 %shard_map.80 = f32[1024,2048]{1,0:T(8,128)} custom-call(f32[1024,768]{1,0:T(8,128)} %get-tuple-element.11.args_0_, f32[1024,768]{1,0:T(8,128)} %shard_map.75.edges.args_1_, f32[1024,1280]{1,0:T(8,128)} %shard_map.77.args_2_, f32[1024,256]{1,0:T(8,128)S(1)} %shard_map.78.args_3_, bf16[256,2048]{1,0:T(8,128)(2,1)S(1)} %get-tuple-element.15.args_4_, ...), custom_call_target="tpu_custom_call" | custom-call | tf_op jit(solution)/shard_map/pallas_call | solution.py:576
  (30 shorter events, 1.2 us)
Async XLA Ops:
  2.9 38.8 %collective-permute-start = (f32[384,768]{1,0:T(8,128)}, f32[384,768]{1,0:T(8,128)S(1)}, u32[]{:S(2)}, u32[]{:S(2)}) collective-permute-start(f32[384,768]{1,0:T(8,128)} %pad_maximum_fusion), channel_id=1, source_target_pairs={{0,4},{4,8},{8,12},{12,16},{16,20},{20,24},{24,28},{1,5},{5,9},{9,... | collective-permute-start | bytes 3538952 | tf_op jit(solution)/shard_map/ppermute | solution.py:34
  6.4 13.0 %copy-start.5 = (s32[8192]{0:T(1024)S(1)}, s32[8192]{0:T(1024)}, u32[]{:S(2)}) copy-start(s32[8192]{0:T(1024)} %param.10) | copy-start | bytes 98308
  6.4 13.0 %copy-start.6 = (s32[8192]{0:T(1024)S(1)}, s32[8192]{0:T(1024)}, u32[]{:S(2)}) copy-start(s32[8192]{0:T(1024)} %param.11) | copy-start | bytes 98308
  6.4 13.0 %copy-start.3 = (f32[8192]{0:T(1024)S(1)}, f32[8192]{0:T(1024)}, u32[]{:S(2)}) copy-start(f32[8192]{0:T(1024)} %param.9) | copy-start | bytes 98308
  6.4 13.0 %copy-start.4 = (f32[8192]{0:T(1024)S(1)}, f32[8192]{0:T(1024)}, u32[]{:S(2)}) copy-start(f32[8192]{0:T(1024)} %param.8) | copy-start | bytes 98308
  6.4 13.5 %copy-start.7 = (s32[256]{0:T(256)S(1)}, s32[256]{0:T(256)}, u32[]{:S(2)}) copy-start(s32[256]{0:T(256)} %param.12) | copy-start | bytes 3076
  6.5 35.2 %collective-permute-start.1 = (f32[384,768]{1,0:T(8,128)}, f32[384,768]{1,0:T(8,128)}, u32[]{:S(2)}, u32[]{:S(2)}) collective-permute-start(f32[384,768]{1,0:T(8,128)} %pad_maximum_fusion.1), channel_id=1, source_target_pairs={{4,0},{8,4},{12,8},{16,12},{20,16},{24,20},{28,24},{5,1},{9,5},{13... | collective-permute-start | bytes 3538952 | tf_op jit(solution)/shard_map/ppermute | solution.py:35
  12.2 226.9 %collective-permute-start.3 = (f32[384,1280]{1,0:T(8,128)}, f32[384,1280]{1,0:T(8,128)}, u32[]{:S(2)}, u32[]{:S(2)}) collective-permute-start(f32[384,1280]{1,0:T(8,128)} %get-tuple-element.25), channel_id=1, source_target_pairs={{4,0},{8,4},{12,8},{16,12},{20,16},{24,20},{28,24},{5,1},{9,5},{13... | collective-permute-start | bytes 5898248 | tf_op jit(solution)/shard_map/ppermute | solution.py:35
  13.5 225.6 %collective-permute-start.2 = (f32[384,1280]{1,0:T(8,128)}, f32[384,1280]{1,0:T(8,128)S(1)}, u32[]{:S(2)}, u32[]{:S(2)}) collective-permute-start(f32[384,1280]{1,0:T(8,128)} %get-tuple-element.26), channel_id=1, source_target_pairs={{0,4},{4,8},{8,12},{12,16},{16,20},{20,24},{24,28},{1,5},{5,9},{9,... | collective-permute-start | bytes 5898248 | tf_op jit(solution)/shard_map/ppermute | solution.py:34
  42.9 8.6 %copy-start.2 = (f32[256]{0:T(256)S(1)}, f32[256]{0:T(256)}, u32[]{:S(2)}) copy-start(f32[256]{0:T(256)} %param.13) | copy-start | bytes 3076
  225.5 10.5 %copy-start = (f32[1024,256]{1,0:T(8,128)}, f32[1024,256]{1,0:T(8,128)S(1)}, u32[]{:S(2)}) copy-start(f32[1024,256]{1,0:T(8,128)S(1)} %get-tuple-element.12.x) | copy-start | bytes 3145732
  225.6 10.5 %collective-permute-start.5 = (f32[384,256]{1,0:T(8,128)S(1)}, f32[384,256]{1,0:T(8,128)S(1)}, u32[]{:S(2)}, u32[]{:S(2)}) collective-permute-start(f32[384,256]{1,0:T(8,128)S(1)} %get-tuple-element.31), channel_id=1, source_target_pairs={{4,0},{8,4},{12,8},{16,12},{20,16},{24,20},{28,24},{5,1},{9,5},{13... | collective-permute-start | bytes 1179656 | tf_op jit(solution)/shard_map/ppermute | solution.py:35
  226.8 9.2 %collective-permute-start.4 = (f32[384,256]{1,0:T(8,128)S(1)}, f32[384,256]{1,0:T(8,128)S(1)}, u32[]{:S(2)}, u32[]{:S(2)}) collective-permute-start(f32[384,256]{1,0:T(8,128)S(1)} %get-tuple-element.32), channel_id=1, source_target_pairs={{0,4},{4,8},{8,12},{12,16},{16,20},{20,24},{24,28},{1,5},{5,9},{9,... | collective-permute-start | bytes 1179656 | tf_op jit(solution)/shard_map/ppermute | solution.py:34
  229.9 1.8 copy-start.1

commit v4 on v3

--- a/solution.py
+++ b/solution.py
@@ -417,21 +417,24 @@
     )
     small = [small_reduce(s_acc, s_rx, s_part, s_part_rx, s_all, first, rest, sems, 0)]
     advance_all(small)
-    wide.start()
     for k in range(tiles):
         a_acc[k * nobs : (k + 1) * nobs, :] = a[:, k * LON : (k + 1) * LON]
     b_acc[...] = b[...]
-    large = [
-        all_reduce(a_acc, a_rx, a_all, row, rows, sems, used),
-        all_reduce(b_acc, b_rx, b_all, col, cols, sems, used + 2 * n_row),
-    ]
+    large = [all_reduce(a_acc, a_rx, a_all, row, rows, sems, used)]
+    other = [all_reduce(b_acc, b_rx, b_all, col, cols, sems, used + 2 * n_row)]
     advance_all(large)
+    advance_all(other)
     step = 0
     while small:
         advance_all(small)
         step += 1
+        if step % 2 == 0:
+            advance_all(other)
         if step % 3 == 0:
             advance_all(large)
+    while other:
+        advance_all(other)
+    wide.start()
     sub = lax.broadcasted_iota(jnp.int32, (nobs, nobs), 0)
     lane = lax.broadcasted_iota(jnp.int32, (nobs, nobs), 1)
     m = s_all[...] + jnp.where(sub == lane, jnp.broadcast_to(r[...], (nobs, nobs)), 0.0)

time: 270 us -> 233 us (0.86)
  Pallas kernels: 225 us -> 189 us
    pallas_call x1, Pallas kernels: 174 us -> 138 us  [sums(): pl.pallas_call(functools.partial(sums_kernel, sizes), in_specs=[vmem] * 5...]
  transfers between devices with their start and end apart: 6 -> 6, of which waited for: 0 -> 0; matrix products, arithmetic and copies ran while one was open for 8% -> 9% of each run, Pallas kernels for 74% -> 70%
where the time goes in v4:
time: 233 us; the launch traced here: 231 us
  Pallas kernels  189 us (81%)
  starting transfers between devices  15.4 us (7%)
  matrix products  14.1 us (6%)
  local copies, waits for them, and re-layouts  9.58 us (4%)
  other arithmetic  2.38 us (1%)
    pallas_call x1, Pallas kernels, sums(): pl.pallas_call(functools.partial(sums_kernel, sizes), in_specs=[vmem] * 5...  138 us
    pallas_call x3, Pallas kernels, row_transport(): pl.pallas_call(functools.partial(row_kernel, rows // LON), grid=(tiles,),...  25 us
    pallas_call x1, Pallas kernels, shards(): pl.pallas_call(functools.partial(final_kernel, pieces, len(arrays)), grid...  14.8 us
    ppermute x3, starting transfers between devices, halos(): lax.ppermute(tail, axis, [(i, i + hop) for i in range(count - hop)])  11.4 us
    pallas_call x2, Pallas kernels, site_rows(): pl.pallas_call(site_kernel, grid_spec=pltpu.PrefetchScalarGridSpec(num_sc...  7.48 us
    dot_general x1, matrix products, shards(): a_part = dot(g_row, covariance, (((1,), (0,)), ((), ())))  6.29 us
    slice x3, local copies, waits for them, and re-layouts, part(): lax.slice_in_dim(x, lo, hi, axis=dim)  6.15 us
    dot_general x1, matrix products, shards(): b_part = dot(covariance, g_col, (((1,), (1,)), ((), ())))  5.91 us
  transfers between devices with their start and end apart: 6, of which 0 were waited for; matrix products, arithmetic and copies ran while one was open for 9% of the time, Pallas kernels for 70%

profile of v4, /device:TPU:0, one launch (start us, length us, event | category | flops | bytes accessed | tf_op | source)
XLA Modules:
  0.0 231.2 jit_solution(5582715233487860760)
XLA Ops:
  0.0 1.8 fusion.6
  1.8 1.1 pad_maximum_fusion
  2.9 2.4 %collective-permute-start = (f32[384,768]{1,0:T(8,128)}, f32[384,768]{1,0:T(8,128)S(1)}, u32[]{:S(2)}, u32[]{:S(2)}) collective-permute-start(f32[384,768]{1,0:T(8,128)} %pad_maximum_fusion), channel_id=1, source_target_pairs={{0,4},{4,8},{8,12},{12,16},{16,20},{20,24},{24,28},{1,5},{5,9},{9,... | collective-permute-start | bytes 3538952 | tf_op jit(solution)/shard_map/ppermute | solution.py:34
  5.3 1.1 pad_maximum_fusion.1
  6.5 1.4 collective-permute-start.1
  7.9 4.3 %fusion.5 = (f32[384,1280]{1,0:T(8,128)}, f32[384,1280]{1,0:T(8,128)}) fusion(f32[1024,2048]{1,0:T(8,128)} %x.5), kind=kLoop, calls=%fused_computation.15 | loop fusion | bytes 7864320 | tf_op jit(solution)/shard_map/slice | solution.py:29
  12.2 1.3 collective-permute-start.3
  13.5 5.9 %collective-permute-start.2 = (f32[384,1280]{1,0:T(8,128)}, f32[384,1280]{1,0:T(8,128)S(1)}, u32[]{:S(2)}, u32[]{:S(2)}) collective-permute-start(f32[384,1280]{1,0:T(8,128)} %get-tuple-element.26), channel_id=1, source_target_pairs={{0,4},{4,8},{8,12},{12,16},{16,20},{20,24},{24,28},{1,5},{5,9},{9,... | collective-permute-start | bytes 5898248 | tf_op jit(solution)/shard_map/ppermute | solution.py:34
  20.1 2.8 %shard_map.73 = f32[256,1024]{1,0:T(8,128)S(1)} custom-call(s32[1]{0:T(128)} %bitcast.start_ref, s32[256,1]{1,0:T(8,128)S(1)} %copy.9.site, f32[1,1792]{1,0:T(1,128)S(1)} %get-tuple-element.42.cu, f32[1,1792]{1,0:T(1,128)S(1)} %get-tuple-element.40.cv, f32[1,1792]{1,0:T(1,128)S(1)} %get-tuple-element.38.su, f32[1,1792]{1,0:T(1,128)S(1)} %get-tuple-element.18.sv), custom_call_target="tpu_custom_call" | custom-call | tf_op jit(solution)/shard_map/pallas_call | solution.py:185
  22.9 4.7 %shard_map.74 = f32[256,2048]{1,0:T(8,128)S(1)} custom-call(s32[1]{0:T(128)} %bitcast.6.start_ref, s32[256,1]{1,0:T(8,128)S(1)} %copy.9.site, f32[1,2816]{1,0:T(1,128)S(1)} %get-tuple-element.36.cu.args_6_, f32[1,2816]{1,0:T(1,128)S(1)} %get-tuple-element.35.cv.args_7_, f32[1,2816]{1,0:T(1,128)S(1)} %get-tuple-element.34.su.args_8_, ...), custom_call_target="tpu_custom_call" | custom-call | tf_op jit(solution)/shard_map/pallas_call | solution.py:185
  27.6 6.3 %fusion.9.a = f32[256,2048]{1,0:T(8,128)S(1)} fusion(f32[256,1024]{1,0:T(8,128)S(1)} %shard_map.73, f32[1024,2048]{1,0:T(8,128)} %x.5), kind=kOutput, calls=%fused_computation.19 | convolution fusion | flops 3221225472 | bytes 11534336 | tf_op jit(solution)/shard_map/dot_general | solution.py:557
  33.9 1.9 fusion.10.s
  35.8 5.9 %convolution_bitcast_fusion.b = f32[1024,256]{1,0:T(8,128)S(1)} fusion(f32[256,2048]{1,0:T(8,128)S(1)} %shard_map.74, f32[1024,2048]{1,0:T(8,128)} %x.5), kind=kOutput, calls=%fused_computation | convolution fusion | flops 3221225472 | bytes 11534336 | tf_op jit(solution)/shard_map/dot_general | solution.py:558
  42.0 0.3 broadcast_in_dim.33.su
  42.3 0.3 broadcast_in_dim.31.cv
  42.9 8.6 %shard_map.75.edges.args_1_ = f32[1024,768]{1,0:T(8,128)} custom-call(f32[1024,2048]{1,0:T(8,128)} %x.5, f32[384,768]{1,0:T(8,128)S(1)} %collective-permute-done.lo, f32[384,768]{1,0:T(8,128)} %collective-permute-done.1.hi, f32[1792,128]{1,0:T(8,128)S(1)} %broadcast_in_dim.29.cu, f32[1792,128]{1,0:T(8,128)S(1)} %broadcast_in_dim.31.cv, ...), custom_call_target="tpu_custom_call" | custom-call | flops 41287680 | bytes 33030144 | tf_op jit(solution)/shard_map/pallas_call | solution.py:78
  51.5 137.9 %shard_map.76 = (f32[256,2816]{1,0:T(8,128)}, f32[1024,256]{1,0:T(8,128)S(1)}, f32[256,256]{1,0:T(8,128)S(1)}, f32[1024,768]{1,0:T(8,128)}) custom-call(f32[256,2048]{1,0:T(8,128)S(1)} %fusion.9.a, f32[1024,256]{1,0:T(8,128)S(1)} %convolution_bitcast_fusion.b, f32[256,256]{1,0:T(8,128)S(1)} %fusion.10.s, f32[1,256]{1,0:T(1,128)S(1)} %bitcast.16, ...), custom_call_target="tpu_custom_call" | custom-call | flops 33554432 | bytes 167772160 | tf_op jit(solution)/shard_map/pallas_call | solution.py:478
  189.5 1.3 collective-permute-start.5
  190.8 3.1 %collective-permute-start.4 = (f32[384,256]{1,0:T(8,128)S(1)}, f32[384,256]{1,0:T(8,128)S(1)}, u32[]{:S(2)}, u32[]{:S(2)}) collective-permute-start(f32[384,256]{1,0:T(8,128)S(1)} %get-tuple-element.32), channel_id=1, source_target_pairs={{0,4},{4,8},{8,12},{12,16},{16,20},{20,24},{24,28},{1,5},{5,9},{9,... | collective-permute-start | bytes 1179656 | tf_op jit(solution)/shard_map/ppermute | solution.py:34
  193.9 1.8 copy-done.1
  195.7 4.3 %shard_map.79 = (bf16[256,2048]{1,0:T(8,128)(2,1)S(1)}, bf16[256,2048]{1,0:T(8,128)(2,1)S(1)}) custom-call(f32[256,2816]{1,0:T(8,128)S(1)} %copy-done.1, f32[256,256]{1,0:T(8,128)S(1)} %get-tuple-element.14.inv, f32[1,2816]{1,0:T(1,128)S(1)} %get-tuple-element.36.cu.args_6_, f32[1,2816]{1,0:T(1,128)S(1)} %get-tuple-element.35.cv.args_7_, ...), custom_call_target="tpu_custom_call" | custom-call | tf_op jit(solution)/shard_map/pallas_call | solution.py:568
  200.0 3.1 %shard_map.78.args_3_ = f32[1024,256]{1,0:T(8,128)S(1)} custom-call(f32[1024,256]{1,0:T(8,128)} %copy-done, f32[384,256]{1,0:T(8,128)S(1)} %collective-permute-done.4.lo, f32[384,256]{1,0:T(8,128)S(1)} %collective-permute-done.5.hi, f32[1792,128]{1,0:T(8,128)S(1)} %broadcast_in_dim.29.cu, f32[1792,128]{1,0:T(8,128)S(1)} %broadcast_in_dim.31.cv, ...), custom_call_target="tpu_custom_call" | custom-call | flops 13762560 | bytes 11010048 | tf_op jit(solution)/shard_map/pallas_call | solution.py:78
  203.2 13.3 %shard_map.77.args_2_ = f32[1024,1280]{1,0:T(8,128)} custom-call(f32[1024,2048]{1,0:T(8,128)} %x.5, f32[384,1280]{1,0:T(8,128)S(1)} %collective-permute-done.2.lo, f32[384,1280]{1,0:T(8,128)} %collective-permute-done.3.hi, f32[1792,128]{1,0:T(8,128)S(1)} %broadcast_in_dim.29.cu, f32[1792,128]{1,0:T(8,128)S(1)} %broadcast_in_dim.31.cv, ...), custom_call_target="tpu_custom_call" | custom-call | flops 68812800 | bytes 55050240 | tf_op jit(solution)/shard_map/pallas_call | solution.py:78
  216.4 14.8 %shard_map.80 = f32[1024,2048]{1,0:T(8,128)} custom-call(f32[1024,768]{1,0:T(8,128)} %get-tuple-element.11.args_0_, f32[1024,768]{1,0:T(8,128)} %shard_map.75.edges.args_1_, f32[1024,1280]{1,0:T(8,128)} %shard_map.77.args_2_, f32[1024,256]{1,0:T(8,128)S(1)} %shard_map.78.args_3_, bf16[256,2048]{1,0:T(8,128)(2,1)S(1)} %get-tuple-element.15.args_4_, ...), custom_call_target="tpu_custom_call" | custom-call | tf_op jit(solution)/shard_map/pallas_call | solution.py:579
  (30 shorter events, 1.2 us)
Async XLA Ops:
  2.9 38.8 %collective-permute-start = (f32[384,768]{1,0:T(8,128)}, f32[384,768]{1,0:T(8,128)S(1)}, u32[]{:S(2)}, u32[]{:S(2)}) collective-permute-start(f32[384,768]{1,0:T(8,128)} %pad_maximum_fusion), channel_id=1, source_target_pairs={{0,4},{4,8},{8,12},{12,16},{16,20},{20,24},{24,28},{1,5},{5,9},{9,... | collective-permute-start | bytes 3538952 | tf_op jit(solution)/shard_map/ppermute | solution.py:34
  6.4 13.0 %copy-start.5 = (s32[8192]{0:T(1024)S(1)}, s32[8192]{0:T(1024)}, u32[]{:S(2)}) copy-start(s32[8192]{0:T(1024)} %param.10) | copy-start | bytes 98308
  6.4 13.0 %copy-start.6 = (s32[8192]{0:T(1024)S(1)}, s32[8192]{0:T(1024)}, u32[]{:S(2)}) copy-start(s32[8192]{0:T(1024)} %param.11) | copy-start | bytes 98308
  6.4 13.0 %copy-start.3 = (f32[8192]{0:T(1024)S(1)}, f32[8192]{0:T(1024)}, u32[]{:S(2)}) copy-start(f32[8192]{0:T(1024)} %param.9) | copy-start | bytes 98308
  6.4 13.0 %copy-start.4 = (f32[8192]{0:T(1024)S(1)}, f32[8192]{0:T(1024)}, u32[]{:S(2)}) copy-start(f32[8192]{0:T(1024)} %param.8) | copy-start | bytes 98308
  6.4 13.5 %copy-start.7 = (s32[256]{0:T(256)S(1)}, s32[256]{0:T(256)}, u32[]{:S(2)}) copy-start(s32[256]{0:T(256)} %param.12) | copy-start | bytes 3076
  6.5 35.2 %collective-permute-start.1 = (f32[384,768]{1,0:T(8,128)}, f32[384,768]{1,0:T(8,128)}, u32[]{:S(2)}, u32[]{:S(2)}) collective-permute-start(f32[384,768]{1,0:T(8,128)} %pad_maximum_fusion.1), channel_id=1, source_target_pairs={{4,0},{8,4},{12,8},{16,12},{20,16},{24,20},{28,24},{5,1},{9,5},{13... | collective-permute-start | bytes 3538952 | tf_op jit(solution)/shard_map/ppermute | solution.py:35
  12.2 190.9 %collective-permute-start.3 = (f32[384,1280]{1,0:T(8,128)}, f32[384,1280]{1,0:T(8,128)}, u32[]{:S(2)}, u32[]{:S(2)}) collective-permute-start(f32[384,1280]{1,0:T(8,128)} %get-tuple-element.25), channel_id=1, source_target_pairs={{4,0},{8,4},{12,8},{16,12},{20,16},{24,20},{28,24},{5,1},{9,5},{13... | collective-permute-start | bytes 5898248 | tf_op jit(solution)/shard_map/ppermute | solution.py:35
  13.5 189.6 %collective-permute-start.2 = (f32[384,1280]{1,0:T(8,128)}, f32[384,1280]{1,0:T(8,128)S(1)}, u32[]{:S(2)}, u32[]{:S(2)}) collective-permute-start(f32[384,1280]{1,0:T(8,128)} %get-tuple-element.26), channel_id=1, source_target_pairs={{0,4},{4,8},{8,12},{12,16},{16,20},{20,24},{24,28},{1,5},{5,9},{9,... | collective-permute-start | bytes 5898248 | tf_op jit(solution)/shard_map/ppermute | solution.py:34
  42.9 8.6 %copy-start.2 = (f32[256]{0:T(256)S(1)}, f32[256]{0:T(256)}, u32[]{:S(2)}) copy-start(f32[256]{0:T(256)} %param.13) | copy-start | bytes 3076
  189.5 10.5 %copy-start = (f32[1024,256]{1,0:T(8,128)}, f32[1024,256]{1,0:T(8,128)S(1)}, u32[]{:S(2)}) copy-start(f32[1024,256]{1,0:T(8,128)S(1)} %get-tuple-element.12.x) | copy-start | bytes 3145732
  189.5 10.5 %collective-permute-start.5 = (f32[384,256]{1,0:T(8,128)S(1)}, f32[384,256]{1,0:T(8,128)S(1)}, u32[]{:S(2)}, u32[]{:S(2)}) collective-permute-start(f32[384,256]{1,0:T(8,128)S(1)} %get-tuple-element.31), channel_id=1, source_target_pairs={{4,0},{8,4},{12,8},{16,12},{20,16},{24,20},{28,24},{5,1},{9,5},{13... | collective-permute-start | bytes 1179656 | tf_op jit(solution)/shard_map/ppermute | solution.py:35
  190.8 9.2 %collective-permute-start.4 = (f32[384,256]{1,0:T(8,128)S(1)}, f32[384,256]{1,0:T(8,128)S(1)}, u32[]{:S(2)}, u32[]{:S(2)}) collective-permute-start(f32[384,256]{1,0:T(8,128)S(1)} %get-tuple-element.32), channel_id=1, source_target_pairs={{0,4},{4,8},{8,12},{12,16},{16,20},{20,24},{24,28},{1,5},{5,9},{9,... | collective-permute-start | bytes 1179656 | tf_op jit(solution)/shard_map/ppermute | solution.py:34
  193.9 1.8 copy-start.1

commit v5 on v4

--- a/solution.py
+++ b/solution.py
@@ -384,9 +384,12 @@
 
 
 def sums_kernel(
-    sizes, a, b, s, r, edges, a_out, b_out, inv_out, beside,
-    a_acc, a_rx, a_all, b_acc, b_rx, b_all, s_acc, s_rx, s_part, s_part_rx, s_all, a_side, sems,
+    sizes, fits, a, b, s, r, beside, a_out, b_out, inv_out, *rest_refs,
 ):
+    corners, scratch = rest_refs[: 2 * fits], rest_refs[2 * fits :]
+    (
+        a_acc, a_rx, a_all, b_acc, b_rx, b_all, s_acc, s_rx, s_part, s_part_rx, s_all, a_side, sems,
+    ) = scratch
     barrier = pltpu.get_barrier_semaphore()
     greeted = 0
     for axis, count in sizes:
@@ -397,12 +400,13 @@
             )
             greeted += 1
     (row, rows), (col, cols) = sizes
-    place = lax.axis_index(col)
-    for near in ((place + 1) % cols, (place + cols - 1) % cols):
-        pl.semaphore_signal(
-            barrier, inc=1, device_id={col: near}, device_id_type=pl.DeviceIdType.MESH
-        )
-        greeted += 1
+    for axis, count in sizes:
+        place = lax.axis_index(axis)
+        for near in ((place + 1) % count, (place + count - 1) % count):
+            pl.semaphore_signal(
+                barrier, inc=1, device_id={axis: near}, device_id_type=pl.DeviceIdType.MESH
+            )
+            greeted += 1
     pl.semaphore_wait(barrier, greeted)
     nobs = s.shape[0]
     tiles = a.shape[1] // LON
@@ -411,10 +415,10 @@
     n_row, n_col = len(powers(rows)), len(powers(cols))
     used = 2 * len(first) + len(rest)
     last = used + 2 * (n_row + n_col)
-    wide = Edges(
-        edges.at[:, :MARGIN], edges.at[:, edges.shape[1] - MARGIN :], beside.at[:, :MARGIN], beside.at[:, MARGIN:],
-        col, cols, sems, last,
-    )
+    wide = None
+    if fits:
+        ends = beside.at[:MARGIN, :], beside.at[beside.shape[0] - MARGIN :, :]
+        wide = Edges(*ends, *corners, row, rows, sems, last)
     small = [small_reduce(s_acc, s_rx, s_part, s_part_rx, s_all, first, rest, sems, 0)]
     advance_all(small)
     for k in range(tiles):
@@ -432,9 +436,9 @@
             advance_all(other)
         if step % 3 == 0:
             advance_all(large)
-    while other:
-        advance_all(other)
-    wide.start()
+    large += other
+    if fits:
+        wide.start()
     sub = lax.broadcasted_iota(jnp.int32, (nobs, nobs), 0)
     lane = lax.broadcasted_iota(jnp.int32, (nobs, nobs), 1)
     m = s_all[...] + jnp.where(sub == lane, jnp.broadcast_to(r[...], (nobs, nobs)), 0.0)
@@ -456,7 +460,8 @@
         c = MARGIN + (tiles + k) * LON
         a_out[:, k * LON : (k + 1) * LON] = a_side[0, k * nobs : (k + 1) * nobs, :]
         a_out[:, c : c + LON] = a_side[1, k * nobs : (k + 1) * nobs, :]
-    wide.finish()
+    if fits:
+        wide.finish()
 
 
 def small_order(sizes):
@@ -466,7 +471,8 @@
     return first, [(row, d) for d in row_powers[1:]]
 
 
-def sums(a, b, s, r, edges):
+def sums(a, b, s, r, beside):
+    fits = beside.shape[0] >= MARGIN
     sizes = [(axis, lax.axis_size(axis)) for axis in ("row", "col")]
     first, rest = small_order(sizes)
     copies = 2 * len(first) + len(rest) + 2 * sum(len(powers(n)) for _, n in sizes) + 4
@@ -476,14 +482,13 @@
     vmem = pl.BlockSpec(memory_space=pltpu.VMEM)
     f32 = jnp.float32
     return pl.pallas_call(
-        functools.partial(sums_kernel, sizes),
+        functools.partial(sums_kernel, sizes, fits),
         in_specs=[vmem] * 5,
-        out_specs=[vmem] * 4,
+        out_specs=[vmem] * (3 + 2 * fits),
         out_shape=[
             jax.ShapeDtypeStruct(shape, f32)
-            for shape in (
-                (nobs, a.shape[1] + 2 * MARGIN), b.shape, s.shape, (b.shape[0], 2 * MARGIN)
-            )
+            for shape in [(nobs, a.shape[1] + 2 * MARGIN), b.shape, s.shape]
+            + [(MARGIN, 2 * MARGIN)] * (2 * fits)
         ],
         scratch_shapes=[
             pltpu.VMEM((tall, LON), f32),
@@ -506,7 +511,7 @@
         cost_estimate=pl.CostEstimate(
             flops=2 * nobs**3, bytes_accessed=80 * a.size * 4, transcendentals=nobs
         ),
-    )(a, b, s, r, edges)
+    )(a, b, s, r, beside)
 
 
 def shards(
@@ -529,25 +534,10 @@
     ]
 
     tiles = cols // LON
-    if tiles > 2 * STEPS:
-        ends = slice(0, MARGIN), slice(cols - MARGIN, cols)
-        edge_lo, edge_hi = halos([covariance[:, c] for c in ends], "row", 0)
-        mid_lo, mid_hi = halos([covariance[:, MARGIN : cols - MARGIN]], "row", 0)
-        skip = tiles - 2 * STEPS
-        edges = row_transport(
-            covariance, edge_lo, edge_hi, row_coeffs, 2 * STEPS,
-            lambda j: jnp.where(j < STEPS, j, j + skip),
-        )
-        middle = row_transport(
-            covariance, mid_lo, mid_hi, row_coeffs, skip, lambda j: j + STEPS
-        )
-        extra = [middle]
-        inner = [(1, 0, STEPS), (2, 0, skip), (1, STEPS, STEPS)]
-    else:
-        edges = row_transport(
-            covariance, *halos([covariance], "row", 0), row_coeffs, tiles, lambda j: j
-        )
-        extra, inner = [], [(1, 0, tiles)]
+    beside = jnp.concatenate(halos([covariance], "col", 1), axis=1)
+    moved = row_transport(
+        covariance, *halos([covariance], "row", 0), row_coeffs, tiles, lambda j: j
+    )
 
     g_row = site_rows(measurement_site_position, row_start, row_lines)
     g_col = site_rows(measurement_site_position, col_start, col_lines)
@@ -559,9 +549,13 @@
     s_part = lax.dot_general(
         a_part, g_col, (((1,), (1,)), ((), ())), precision=HIGHEST, preferred_element_type=jnp.float32
     )
-    a, b, inv, beside = sums(a_part, b_part, s_part, obs_var.reshape(1, nobs), edges)
-    arrays = [beside, edges] + extra
-    pieces = [(0, 0, STEPS)] + inner + [(0, STEPS, STEPS)]
+    a_part, b_part, s_part, moved = lax.optimization_barrier((a_part, b_part, s_part, moved))
+    a, b, inv, *corners = sums(a_part, b_part, s_part, obs_var.reshape(1, nobs), beside)
+    if not corners:
+        corners = halos([beside], "row", 0)
+    beside = row_transport(beside, *corners, row_coeffs, 2 * STEPS, lambda j: j)
+    arrays = [beside, moved]
+    pieces = [(0, 0, STEPS), (1, 0, tiles), (0, STEPS, STEPS)]
     b_lo, b_hi = halos([b], "row", 0)
     pht = row_transport(b, b_lo, b_hi, row_coeffs, nobs // LON, lambda j: j)
     wide = cols + 2 * MARGIN

time: 233 us -> 255 us (1.094)
  Pallas kernels: 189 us -> 206 us
  local copies, waits for them, and re-layouts: 9.58 us -> 16.7 us
  starting transfers between devices: 15.4 us -> 18.3 us
    pallas_call x1, Pallas kernels: 138 us -> 147 us  [sums(): pl.pallas_call(functools.partial(sums_kernel, sizes, fits), in_specs=[vme...]
    pallas_call x3, Pallas kernels: 25 us -> 32.4 us  [row_transport(): pl.pallas_call(functools.partial(row_kernel, rows // LON), grid=(tiles,),...]
    slice x3, local copies, waits for them, and re-layouts: 6.15 us -> 10.2 us  [part(): lax.slice_in_dim(x, lo, hi, axis=dim)]
    ppermute x3, starting transfers between devices: 11.4 us -> 14.5 us  [halos(): lax.ppermute(tail, axis, [(i, i + hop) for i in range(count - hop)])]
  transfers between devices with their start and end apart: 6 -> 6, of which waited for: 0 -> 1; matrix products, arithmetic and copies ran while one was open for 9% -> 9% of each run, Pallas kernels for 70% -> 8%
where the time goes in v5:
time: 255 us; the launch traced here: 254 us
  Pallas kernels  206 us (81%)
  starting transfers between devices  18.3 us (7%)
  local copies, waits for them, and re-layouts  16.7 us (7%)
  matrix products  11.8 us (5%)
    pallas_call x1, Pallas kernels, sums(): pl.pallas_call(functools.partial(sums_kernel, sizes, fits), in_specs=[vme...  147 us
    pallas_call x3, Pallas kernels, row_transport(): pl.pallas_call(functools.partial(row_kernel, rows // LON), grid=(tiles,),...  32.4 us
    pallas_call x1, Pallas kernels, shards(): pl.pallas_call(functools.partial(final_kernel, pieces, len(arrays)), grid...  14.9 us
    ppermute x3, starting transfers between devices, halos(): lax.ppermute(tail, axis, [(i, i + hop) for i in range(count - hop)])  14.5 us
    slice x3, local copies, waits for them, and re-layouts, part(): lax.slice_in_dim(x, lo, hi, axis=dim)  10.2 us
    pallas_call x2, Pallas kernels, site_rows(): pl.pallas_call(site_kernel, grid_spec=pltpu.PrefetchScalarGridSpec(num_sc...  7.48 us
    dot_general x1, matrix products, shards(): a_part = dot(g_row, covariance, (((1,), (0,)), ((), ())))  6.43 us
  transfers between devices with their start and end apart: 6, of which 1 were waited for; matrix products, arithmetic and copies ran while one was open for 9% of the time, Pallas kernels for 8%

profile of v5, /device:TPU:0, one launch (start us, length us, event | category | flops | bytes accessed | tf_op | source)
XLA Modules:
  0.0 253.9 jit_solution(17534962647539384394)
XLA Ops:
  0.0 3.8 %fusion.6 = (f32[1024,384]{1,0:T(8,128)}, f32[1024,384]{1,0:T(8,128)}) fusion(f32[1024,2048]{1,0:T(8,128)} %x.3), kind=kLoop, calls=%fused_computation.16 | loop fusion | bytes 6291456 | tf_op jit(solution)/shard_map/slice | solution.py:29
  3.8 1.3 collective-permute-start.1
  5.1 6.8 %collective-permute-start = (f32[1024,384]{1,0:T(8,128)}, f32[1024,384]{1,0:T(8,128)}, u32[]{:S(2)}, u32[]{:S(2)}) collective-permute-start(f32[1024,384]{1,0:T(8,128)} %get-tuple-element.38), channel_id=1, source_target_pairs={{0,1},{1,2},{2,3},{4,5},{5,6},{6,7},{8,9},{9,10},{10,11},{12,13},{... | collective-permute-start | bytes 4718600 | tf_op jit(solution)/shard_map/ppermute | solution.py:34
  11.9 6.3 %fusion.5 = (f32[384,2048]{1,0:T(8,128)}, f32[384,2048]{1,0:T(8,128)}) fusion(f32[1024,2048]{1,0:T(8,128)} %x.3), kind=kLoop, calls=%fused_computation.15 | loop fusion | bytes 12582912 | tf_op jit(solution)/shard_map/slice | solution.py:29
  18.2 1.3 collective-permute-start.3
  19.5 4.7 %collective-permute-start.2 = (f32[384,2048]{1,0:T(8,128)}, f32[384,2048]{1,0:T(8,128)}, u32[]{:S(2)}, u32[]{:S(2)}) collective-permute-start(f32[384,2048]{1,0:T(8,128)} %get-tuple-element.36), channel_id=1, source_target_pairs={{0,4},{4,8},{8,12},{12,16},{16,20},{20,24},{24,28},{1,5},{5,9},{9,... | collective-permute-start | bytes 9437192 | tf_op jit(solution)/shard_map/ppermute | solution.py:34
  24.8 2.8 %shard_map.73 = f32[256,1024]{1,0:T(8,128)S(1)} custom-call(s32[1]{0:T(128)} %bitcast.start_ref, s32[256,1]{1,0:T(8,128)S(1)} %copy.9.site, f32[1,1792]{1,0:T(1,128)S(1)} %get-tuple-element.50.cu, f32[1,1792]{1,0:T(1,128)S(1)} %get-tuple-element.48.cv, f32[1,1792]{1,0:T(1,128)S(1)} %get-tuple-element.46.su, f32[1,1792]{1,0:T(1,128)S(1)} %get-tuple-element.28.sv), custom_call_target="tpu_custom_call" | custom-call | tf_op jit(solution)/shard_map/pallas_call | solution.py:185
  27.6 4.7 %shard_map.74 = f32[256,2048]{1,0:T(8,128)S(1)} custom-call(s32[1]{0:T(128)} %bitcast.6.start_ref, s32[256,1]{1,0:T(8,128)S(1)} %copy.9.site, f32[1,2816]{1,0:T(1,128)S(1)} %get-tuple-element.44.cu.args_5_, f32[1,2816]{1,0:T(1,128)S(1)} %get-tuple-element.43.cv.args_6_, f32[1,2816]{1,0:T(1,128)S(1)} %get-tuple-element.42.su.args_7_, ...), custom_call_target="tpu_custom_call" | custom-call | tf_op jit(solution)/shard_map/pallas_call | solution.py:185
  32.3 6.4 %fusion.9.a = f32[256,2048]{1,0:T(8,128)S(1)} fusion(f32[256,1024]{1,0:T(8,128)S(1)} %shard_map.73, f32[1024,2048]{1,0:T(8,128)} %x.3), kind=kOutput, calls=%fused_computation.19 | convolution fusion | flops 3221225472 | bytes 11534336 | tf_op jit(solution)/shard_map/dot_general | solution.py:547
  38.8 1.9 fusion.10.s
  40.7 3.5 %convolution_bitcast_fusion.b = f32[1024,256]{1,0:T(8,128)S(1)} fusion(f32[256,2048]{1,0:T(8,128)S(1)} %shard_map.74, f32[1024,2048]{1,0:T(8,128)S(1)} %bitcast.18), kind=kOutput, calls=%fused_computation | convolution fusion | flops 3221225472 | bytes 11534336 | tf_op jit(solution)/shard_map/dot_general | solution.py:548
  44.2 0.5 collective-permute-done
  44.7 1.5 constant_dynamic-update-slice_fusion.1
  46.2 1.5 constant_dynamic-update-slice_fusion.beside.x
  48.1 0.3 broadcast_in_dim.33.su
  49.0 20.8 %shard_map.75.args_1_ = f32[1024,2048]{1,0:T(8,128)} custom-call(f32[1024,2048]{1,0:T(8,128)} %x.3, f32[384,2048]{1,0:T(8,128)} %collective-permute-done.2.lo, f32[384,2048]{1,0:T(8,128)} %collective-permute-done.3.hi, f32[1792,128]{1,0:T(8,128)S(1)} %broadcast_in_dim.29.cu, f32[1792,128]{1,0:T(8,128)S(1)} %broadcast_in_dim.31.cv, ...), custom_call_target="tpu_custom_call" | custom-call | flops 110100480 | bytes 88080384 | tf_op jit(solution)/shard_map/pallas_call | solution.py:78
  69.8 147.1 %shard_map.76 = (f32[256,2816]{1,0:T(8,128)}, f32[1024,256]{1,0:T(8,128)S(1)}, f32[256,256]{1,0:T(8,128)S(1)}, f32[384,768]{1,0:T(8,128)S(1)}, f32[384,768]{1,0:T(8,128)S(1)}) custom-call(f32[256,2048]{1,0:T(8,128)} %copy-done.4, f32[1024,256]{1,0:T(8,128)S(1)} %convolution_bitcast_fusion.b, f32[256,256]{1,0:T(8,128)S(1)} %fusion.10.s, ...), custom_call_target="tpu_custom_call" | custom-call | flops 33554432 | bytes 167772160 | tf_op jit(solution)/shard_map/pallas_call | solution.py:484
  217.0 1.3 collective-permute-start.5
  218.3 3.1 %collective-permute-start.4 = (f32[384,256]{1,0:T(8,128)S(1)}, f32[384,256]{1,0:T(8,128)S(1)}, u32[]{:S(2)}, u32[]{:S(2)}) collective-permute-start(f32[384,256]{1,0:T(8,128)S(1)} %get-tuple-element.40), channel_id=1, source_target_pairs={{0,4},{4,8},{8,12},{12,16},{16,20},{20,24},{24,28},{1,5},{5,9},{9,... | collective-permute-start | bytes 1179656 | tf_op jit(solution)/shard_map/ppermute | solution.py:34
  221.4 1.8 copy-done.1
  223.2 4.3 %shard_map.79 = (bf16[256,2048]{1,0:T(8,128)(2,1)S(1)}, bf16[256,2048]{1,0:T(8,128)(2,1)S(1)}) custom-call(f32[256,2816]{1,0:T(8,128)S(1)} %copy-done.1, f32[256,256]{1,0:T(8,128)S(1)} %get-tuple-element.24.inv, f32[1,2816]{1,0:T(1,128)S(1)} %get-tuple-element.44.cu.args_5_, f32[1,2816]{1,0:T(1,128)S(1)} %get-tuple-element.43.cv.args_6_, ...), custom_call_target="tpu_custom_call" | custom-call | tf_op jit(solution)/shard_map/pallas_call | solution.py:562
  227.5 8.5 %shard_map.77.args_0_ = f32[1024,768]{1,0:T(8,128)} custom-call(f32[1024,768]{1,0:T(8,128)} %copy-done.3, f32[384,768]{1,0:T(8,128)S(1)} %get-tuple-element.19.lo, f32[384,768]{1,0:T(8,128)S(1)} %get-tuple-element.20.hi, f32[1792,128]{1,0:T(8,128)S(1)} %broadcast_in_dim.29.cu, f32[1792,128]{1,0:T(8,128)S(1)} %broadcast_in_dim.31.cv, ...), custom_call_target="tpu_custom_call" | custom-call | flops 41287680 | bytes 33030144 | tf_op jit(solution)/shard_map/pallas_call | solution.py:78
  236.0 3.1 %shard_map.78.args_2_ = f32[1024,256]{1,0:T(8,128)S(1)} custom-call(f32[1024,256]{1,0:T(8,128)} %copy-done, f32[384,256]{1,0:T(8,128)S(1)} %collective-permute-done.4.lo, f32[384,256]{1,0:T(8,128)S(1)} %collective-permute-done.5.hi, f32[1792,128]{1,0:T(8,128)S(1)} %broadcast_in_dim.29.cu, f32[1792,128]{1,0:T(8,128)S(1)} %broadcast_in_dim.31.cv, ...), custom_call_target="tpu_custom_call" | custom-call | flops 13762560 | bytes 11010048 | tf_op jit(solution)/shard_map/pallas_call | solution.py:78
  239.1 14.9 %shard_map.80 = f32[1024,2048]{1,0:T(8,128)} custom-call(f32[1024,768]{1,0:T(8,128)} %shard_map.77.args_0_, f32[1024,2048]{1,0:T(8,128)} %shard_map.75.args_1_, f32[1024,256]{1,0:T(8,128)S(1)} %shard_map.78.args_2_, bf16[256,2048]{1,0:T(8,128)(2,1)S(1)} %get-tuple-element.25.args_3_, bf16[256,2048]{1,0:T(8,128)(2,1)S(1)} %get-tuple-element.26.args_4_, ...), custom_call_target="tpu_custom_call" | custom-call | tf_op jit(solution)/shard_map/pallas_call | solution.py:573
  (39 shorter events, 1.6 us)
Async XLA Ops:
  3.8 42.4 %collective-permute-start.1 = (f32[1024,384]{1,0:T(8,128)}, f32[1024,384]{1,0:T(8,128)}, u32[]{:S(2)}, u32[]{:S(2)}) collective-permute-start(f32[1024,384]{1,0:T(8,128)} %get-tuple-element.37), channel_id=1, source_target_pairs={{1,0},{2,1},{3,2},{5,4},{6,5},{7,6},{9,8},{10,9},{11,10},{13,12},{... | collective-permute-start | bytes 4718600 | tf_op jit(solution)/shard_map/ppermute | solution.py:35
  5.0 19.1 %copy-start.7 = (s32[8192]{0:T(1024)S(1)}, s32[8192]{0:T(1024)}, u32[]{:S(2)}) copy-start(s32[8192]{0:T(1024)} %param.10) | copy-start | bytes 98308
  5.1 19.1 %copy-start.8 = (s32[8192]{0:T(1024)S(1)}, s32[8192]{0:T(1024)}, u32[]{:S(2)}) copy-start(s32[8192]{0:T(1024)} %param.11) | copy-start | bytes 98308
  5.1 19.1 %copy-start.5 = (f32[8192]{0:T(1024)S(1)}, f32[8192]{0:T(1024)}, u32[]{:S(2)}) copy-start(f32[8192]{0:T(1024)} %param.9) | copy-start | bytes 98308
  5.1 19.1 %copy-start.6 = (f32[8192]{0:T(1024)S(1)}, f32[8192]{0:T(1024)}, u32[]{:S(2)}) copy-start(f32[8192]{0:T(1024)} %param.8) | copy-start | bytes 98308
  5.1 19.4 %copy-start.9 = (s32[256]{0:T(256)S(1)}, s32[256]{0:T(256)}, u32[]{:S(2)}) copy-start(s32[256]{0:T(256)} %param.12) | copy-start | bytes 3076
  5.1 39.6 %collective-permute-start = (f32[1024,384]{1,0:T(8,128)}, f32[1024,384]{1,0:T(8,128)}, u32[]{:S(2)}, u32[]{:S(2)}) collective-permute-start(f32[1024,384]{1,0:T(8,128)} %get-tuple-element.38), channel_id=1, source_target_pairs={{0,1},{1,2},{2,3},{4,5},{5,6},{6,7},{8,9},{9,10},{10,11},{12,13},{... | collective-permute-start | bytes 4718600 | tf_op jit(solution)/shard_map/ppermute | solution.py:34
  18.2 29.6 %collective-permute-start.3 = (f32[384,2048]{1,0:T(8,128)}, f32[384,2048]{1,0:T(8,128)}, u32[]{:S(2)}, u32[]{:S(2)}) collective-permute-start(f32[384,2048]{1,0:T(8,128)} %get-tuple-element.35), channel_id=1, source_target_pairs={{4,0},{8,4},{12,8},{16,12},{20,16},{24,20},{28,24},{5,1},{9,5},{13... | collective-permute-start | bytes 9437192 | tf_op jit(solution)/shard_map/ppermute | solution.py:35
  19.5 28.3 %collective-permute-start.2 = (f32[384,2048]{1,0:T(8,128)}, f32[384,2048]{1,0:T(8,128)}, u32[]{:S(2)}, u32[]{:S(2)}) collective-permute-start(f32[384,2048]{1,0:T(8,128)} %get-tuple-element.36), channel_id=1, source_target_pairs={{0,4},{4,8},{8,12},{12,16},{16,20},{20,24},{24,28},{1,5},{5,9},{9,... | collective-permute-start | bytes 9437192 | tf_op jit(solution)/shard_map/ppermute | solution.py:34
  27.6 13.0 %slice-start = ((s8[8388608]{0:T(1024)(128)(4,1)}), s8[4194304]{0:T(1024)(128)(4,1)S(1)}, s32[]{:S(2)}) async-start(s8[8388608]{0:T(1024)(128)(4,1)} %bitcast.17), calls=%async_computation | async-start | bytes 8388608
  32.3 8.4 %slice-start.1 = ((s8[8388608]{0:T(1024)(128)(4,1)}), s8[4194304]{0:T(1024)(128)(4,1)S(1)}, s32[]{:S(2)}) async-start(s8[8388608]{0:T(1024)(128)(4,1)} %bitcast.17), calls=%async_computation.1 | async-start | bytes 8388608
  38.8 5.4 %copy-start.4 = (f32[256,2048]{1,0:T(8,128)}, f32[256,2048]{1,0:T(8,128)S(1)}, u32[]{:S(2)}) copy-start(f32[256,2048]{1,0:T(8,128)S(1)} %fusion.9.a) | copy-start | bytes 6291460
  47.7 22.1 %copy-start.3 = (f32[1024,768]{1,0:T(8,128)}, f32[1024,768]{1,0:T(8,128)S(1)}, u32[]{:S(2)}) copy-start(f32[1024,768]{1,0:T(8,128)S(1)} %constant_dynamic-update-slice_fusion.beside.x) | copy-start | bytes 9437188
  49.0 20.8 %copy-start.2 = (f32[256]{0:T(256)S(1)}, f32[256]{0:T(256)}, u32[]{:S(2)}) copy-start(f32[256]{0:T(256)} %param.13) | copy-start | bytes 3076
  217.0 19.0 %copy-start = (f32[1024,256]{1,0:T(8,128)}, f32[1024,256]{1,0:T(8,128)S(1)}, u32[]{:S(2)}) copy-start(f32[1024,256]{1,0:T(8,128)S(1)} %get-tuple-element.22.x) | copy-start | bytes 3145732
  217.0 18.9 %collective-permute-start.5 = (f32[384,256]{1,0:T(8,128)S(1)}, f32[384,256]{1,0:T(8,128)S(1)}, u32[]{:S(2)}, u32[]{:S(2)}) collective-permute-start(f32[384,256]{1,0:T(8,128)S(1)} %get-tuple-element.39), channel_id=1, source_target_pairs={{4,0},{8,4},{12,8},{16,12},{20,16},{24,20},{28,24},{5,1},{9,5},{13... | collective-permute-start | bytes 1179656 | tf_op jit(solution)/shard_map/ppermute | solution.py:35
  218.3 17.6 %collective-permute-start.4 = (f32[384,256]{1,0:T(8,128)S(1)}, f32[384,256]{1,0:T(8,128)S(1)}, u32[]{:S(2)}, u32[]{:S(2)}) collective-permute-start(f32[384,256]{1,0:T(8,128)S(1)} %get-tuple-element.40), channel_id=1, source_target_pairs={{0,4},{4,8},{8,12},{12,16},{16,20},{20,24},{24,28},{1,5},{5,9},{9,... | collective-permute-start | bytes 1179656 | tf_op jit(solution)/shard_map/ppermute | solution.py:34
  221.4 1.8 copy-start.1
